TPU v7x, 32 devices: a whole 2x2x4 slice. The times are simulated.
32 devices in a mesh: lat: 4 (over z), lon: 8 (over y, x, core).
Axes of the slice: x: 2, y: 2, z: 4, core: 2. Of those that a mesh axis runs over, the one named last changes fastest.
Arguments:
- mlp_input: bfloat16 [128, 384, 640], P('lat', 'lon'), may hold values from -6 to 6
- out_cot: bfloat16 [128, 384, 640], P('lat', 'lon'), may hold values from -6 to 6
- w_in: bfloat16 [640, 1280], replicated, may hold values from -0.25 to 0.25
- w_out: bfloat16 [1280, 640], replicated, may hold values from -0.15625 to 0.15625
- chan_weights: float32 [9, 640], replicated, may hold values from -2 to 2
- row_weights: float32 [9, 128, 9], replicated, may hold values from -2 to 2
- basis_spectra: float32 [9, 384], replicated, may hold values from -6 to 6
- band_cols: int32 [128, 9], replicated, may hold values from 0 to 127, as said below
- band_widths: int32 [128], replicated, may hold values from 1 to 9, as said below
Outputs:
- grid_grad: bfloat16 [128, 384, 640], P('lat', 'lon')
- grad_in: float32 [640, 1280], P('lat', 'lon')
- grad_out: float32 [1280, 640], P('lon', 'lat')
Inputs may be any that keep to these rules, and one draw needn't show every extreme that they name: `band_cols`: slot 0 of each row is the row itself; every slot lies within 4 rows of its own row. `band_widths`: the 4 rows nearest each pole use all 9 slots; slots at or beyond a row's width are padding.
All inputs are finite; a program needn't handle non-finite values.
Results may differ from a plain program's by a relative error of at most 0.02.
Values may be sent and summed in bfloat16 or wider, within the bound.
A program may use at most 128 MiB of HBM per device.

v0:
```python
import functools
import math

import jax
import jax.numpy as jnp
import numpy as np
from jax import lax
from jax.experimental import pallas as pl
from jax.experimental.pallas import tpu as pltpu
from jax.sharding import PartitionSpec as P


def padded(cells, sides, width):
    for axis, dim in sides:
        count = lax.axis_size(axis)
        ends = count - 1
        head = lax.slice_in_dim(cells, 0, width, axis=dim)
        tail = lax.slice_in_dim(cells, cells.shape[dim] - width, cells.shape[dim], axis=dim)
        cells = jnp.concatenate(
            [
                lax.ppermute(tail, axis, [(i, (i + 1) % count) for i in range(ends)]),
                cells,
                lax.ppermute(head, axis, [((i + 1) % count, i) for i in range(ends)]),
            ],
            axis=dim,
        )
    return cells


def gelu_parts(pre_act):
    inner_arg = 0.7978845608 * (pre_act + 0.044715 * pre_act * pre_act * pre_act)
    tangent = jnp.tanh(inner_arg)
    gelu_value = 0.5 * pre_act * (1.0 + tangent)
    gelu_slope = 0.5 * (1.0 + tangent) + 0.5 * pre_act * (
        1.0 - tangent * tangent
    ) * 0.7978845608 * (1.0 + 0.134145 * pre_act * pre_act)
    return (gelu_value, gelu_slope)


def tables(lon_total):
    half_len = lon_total // 2
    lon_index = jnp.arange(lon_total, dtype=jnp.int32)
    frequency = jnp.arange(2 * half_len, dtype=jnp.int32) % half_len
    phases = lon_index[:, None] * frequency[None, :] % lon_total
    angles = phases.astype(jnp.float32) * jnp.float32(2.0 * math.pi / lon_total)
    is_sine = jnp.arange(2 * half_len, dtype=jnp.int32) >= half_len
    forward = jnp.where(is_sine[None, :], jnp.sin(angles), jnp.cos(angles))
    scaling = jnp.where(frequency == 0, jnp.float32(1.0), jnp.float32(2.0)) / jnp.float32(lon_total)
    inverse = forward.T * scaling[:, None]
    return (forward, inverse)


def weighted(spectra, basis_spectra, chan_w):
    half_len = spectra.shape[-1] // 2
    real_part = spectra[..., :half_len]
    imag_part = spectra[..., half_len:]
    cosine = basis_spectra[:, None, None, :half_len]
    sine = basis_spectra[:, None, None, half_len:]
    first = cosine * real_part[None] + sine * imag_part[None]
    second = cosine * imag_part[None] - sine * real_part[None]
    return jnp.concatenate([first, second], -1) * chan_w[:, None, :, None]


def contract_tokens(left, right):
    return lax.dot_general(
        left, right, (((0,), (0,)), ((), ())), preferred_element_type=jnp.float32
    )


def body(
    mlp_input,
    out_cot,
    w_in,
    w_out,
    chan_weights,
    row_weights,
    basis_spectra,
    band_cols,
    band_widths,
):
    lat_rows, lon_cols, channels = mlp_input.shape
    lon_shards = lax.axis_size("lon")
    local_chans = channels // lon_shards
    lon_total = lon_cols * lon_shards
    band_slots = row_weights.shape[2]
    band_reach = (band_slots - 1) // 2
    row_start = lax.axis_index("lat") * lat_rows
    chan_start = lax.axis_index("lon") * local_chans
    tokens = mlp_input.reshape(lat_rows * lon_cols, channels)
    cotangent = out_cot.reshape(lat_rows * lon_cols, channels)
    pre_act = jnp.dot(tokens, w_in, preferred_element_type=jnp.float32)
    gelu_value, gelu_slope = gelu_parts(pre_act)
    hidden = gelu_value.astype(jnp.bfloat16)
    back_proj = lax.dot_general(
        cotangent, w_out, (((1,), (1,)), ((), ())), preferred_element_type=jnp.float32
    )
    pre_grad = (back_proj * gelu_slope).astype(jnp.bfloat16)
    input_back = lax.dot_general(
        pre_grad, w_in, (((1,), (1,)), ((), ())), preferred_element_type=jnp.float32
    )
    grid_cot = (
        (cotangent.astype(jnp.float32) + input_back)
        .astype(jnp.bfloat16)
        .reshape(lat_rows, lon_cols, channels)
    )
    part_in = lax.optimization_barrier(
        contract_tokens(tokens, pre_grad).astype(jnp.bfloat16)
    ).astype(jnp.float32)
    part_out = lax.optimization_barrier(
        contract_tokens(hidden, cotangent).astype(jnp.bfloat16)
    ).astype(jnp.float32)
    half_in, half_out = (
        lax.psum_scatter(
            part_in.astype(jnp.bfloat16), "lon", scatter_dimension=1, tiled=True
        ).astype(jnp.float32),
        lax.psum_scatter(
            part_out.astype(jnp.bfloat16), "lon", scatter_dimension=0, tiled=True
        ).astype(jnp.float32),
    )
    grad_in, grad_out = (
        lax.psum_scatter(half_in, "lat", scatter_dimension=0, tiled=True),
        lax.psum_scatter(half_out, "lat", scatter_dimension=1, tiled=True),
    )
    chan_w = lax.dynamic_slice_in_dim(chan_weights, chan_start, local_chans, 1)
    forward, inverse = tables(lon_total)
    slot_index = jnp.arange(band_slots, dtype=jnp.int32)
    src_cols = lax.dynamic_slice_in_dim(band_cols, row_start, lat_rows, 0)
    src_widths = lax.dynamic_slice_in_dim(band_widths, row_start, lat_rows, 0)
    src_coeffs = lax.dynamic_slice_in_dim(row_weights, row_start, lat_rows, 1)
    target = src_cols - (row_start - band_reach)
    target_count = lat_rows + 2 * band_reach
    moved = lax.all_to_all(
        grid_cot.reshape(lat_rows, lon_cols, lon_shards, local_chans),
        "lon",
        split_axis=2,
        concat_axis=1,
        tiled=True,
    )
    spectra = jnp.einsum(
        "rlc,lg->rcg",
        moved[:, :, 0, :].astype(jnp.float32),
        forward,
        precision=lax.Precision.HIGHEST,
    )
    mixed = weighted(spectra, basis_spectra, chan_w)
    live_slot = slot_index[None, :] < src_widths[:, None]
    onehot = (
        (target[:, :, None] == jnp.arange(target_count, dtype=jnp.int32)[None, None, :])
        & live_slot[:, :, None]
    ).astype(jnp.float32)
    band_mat = jnp.einsum("koj,ojt->kto", src_coeffs, onehot, precision=lax.Precision.HIGHEST)
    summed = jnp.einsum("kto,kocg->tcg", band_mat, mixed, precision=lax.Precision.HIGHEST)
    rim_rows = jnp.concatenate([summed[:band_reach], summed[lat_rows + band_reach :]], 0)
    received = padded(rim_rows, (("lat", 0),), band_reach)
    own_rows = summed[band_reach : band_reach + lat_rows]
    own_rows = own_rows.at[:band_reach].add(received[:band_reach])
    own_rows = own_rows.at[lat_rows - band_reach :].add(received[3 * band_reach :])
    backed = jnp.einsum("tcg,gl->tlc", own_rows, inverse, precision=lax.Precision.HIGHEST).astype(
        jnp.bfloat16
    )
    returned = lax.all_to_all(
        backed.reshape(lat_rows, lon_total, 1, local_chans),
        "lon",
        split_axis=1,
        concat_axis=2,
        tiled=True,
    )
    returned = returned.reshape(lat_rows, lon_cols, channels)
    grid_grad = (out_cot.astype(jnp.float32) + returned.astype(jnp.float32)).astype(jnp.bfloat16)
    return (grid_grad, grad_in, grad_out)


MESH = pl.DeviceIdType.MESH
ROWS = 8
LANES = 128
SLOPE = 0.7978845608


def nn(left, right):
    return lax.dot_general(left, right, (((1,), (0,)), ((), ())), preferred_element_type=jnp.float32)


def nt(left, right):
    return lax.dot_general(left, right, (((1,), (1,)), ((), ())), preferred_element_type=jnp.float32)


def tn(left, right):
    return lax.dot_general(left, right, (((0,), (0,)), ((), ())), preferred_element_type=jnp.float32)


def swap_blocks(blocks, width):
    count = blocks[0].shape[1] // width
    return [
        jnp.concatenate([block[:, at * width : (at + 1) * width] for block in blocks], axis=1)
        for at in range(count)
    ]


def greet(lat, lon, peers, lat_count):
    barrier = pltpu.get_barrier_semaphore()
    for step in range(1, peers):
        pl.semaphore_signal(
            barrier, inc=1, device_id=(lat, lax.rem(lon + step, peers)), device_id_type=MESH
        )
    if lat_count:
        for step in (1, lat_count - 1):
            pl.semaphore_signal(
                barrier, inc=1, device_id=(lax.rem(lat + step, lat_count), lon), device_id_type=MESH
            )
    pl.semaphore_wait(barrier, peers + 1 if lat_count else peers - 1)


def mlp_kernel(
    peers, cols, chunks,
    tok_hbm, cot_hbm, win_hbm, wout_hbm,
    moved, part_in, part_out,
    tok, cot, win, wout, tok_t, cot_t, hidden, grad, packed, load_sem, send_sem, recv_sem,
):
    lat, lon = lax.axis_index("lat"), lax.axis_index("lon")
    span = ROWS * cols
    tile = 256
    hid = win.shape[1]
    loads = [
        pltpu.make_async_copy(win_hbm, win, load_sem.at[0]),
        pltpu.make_async_copy(wout_hbm, wout, load_sem.at[1]),
    ]
    for i in range(chunks):
        rows = pl.ds(i * span, span)
        loads.append(pltpu.make_async_copy(tok_hbm.at[rows], tok.at[rows], load_sem.at[2 + 2 * i]))
        loads.append(pltpu.make_async_copy(cot_hbm.at[rows], cot.at[rows], load_sem.at[3 + 2 * i]))
    for load in loads:
        load.start()
    greet(lat, lon, peers, 0)
    loads[0].wait()
    loads[1].wait()

    def send(i, peer):
        return pltpu.make_async_remote_copy(
            src_ref=packed.at[i, pl.ds(peer * cols, cols)],
            dst_ref=moved.at[i, pl.ds(lon * cols, cols)],
            send_sem=send_sem.at[i, peer],
            recv_sem=recv_sem.at[i, lon],
            device_id=(lat, peer),
            device_id_type=MESH,
        )

    def own(i):
        rows = pl.ds(lon * cols, cols)
        return pltpu.make_async_copy(packed.at[i, rows], moved.at[i, rows], send_sem.at[i, lon])

    for i in range(chunks):
        rows = pl.ds(i * span, span)
        loads[2 + 2 * i].wait()
        loads[3 + 2 * i].wait()
        here, cotan = tok[rows, :], cot[rows, :]

        def column(j, carry):
            at = pl.ds(pl.multiple_of(j * tile, tile), tile)
            value = nn(here, win[:, at])
            back = nt(cotan, wout[at, :])
            square = value * value
            scaled = SLOPE * value
            tangent = jnp.tanh(scaled * (1.0 + 0.044715 * square))
            gate = 0.5 + 0.5 * tangent
            slope = gate * (1.0 + (1.0 - tangent) * (scaled * (1.0 + 0.134145 * square)))
            hidden[rows, at] = (value * gate).astype(jnp.bfloat16)
            grad[rows, at] = (back * slope).astype(jnp.bfloat16)
            return carry

        lax.fori_loop(0, hid // tile, column, 0)
        grid = (cotan.astype(jnp.float32) + nt(grad[rows, :], win[...])).astype(jnp.bfloat16)
        blocks = [grid[r * cols : (r + 1) * cols] for r in range(ROWS)]
        for at, block in enumerate(swap_blocks(blocks, grid.shape[1] // peers)):
            packed[i, at * cols : (at + 1) * cols, :] = block
        for step in range(1, peers):
            send(i, lax.rem(lon + step, peers)).start()
        own(i).start()
        tok_t[:, i * span : (i + 1) * span] = here.T
        cot_t[:, i * span : (i + 1) * span] = cotan.T

    def products(j, carry):
        at = pl.ds(pl.multiple_of(j * tile, tile), tile)
        part_in[:, at] = nn(tok_t[...], grad[:, at]).astype(jnp.bfloat16)
        part_out[:, at] = nn(cot_t[...], hidden[:, at]).astype(jnp.bfloat16)
        return carry

    lax.fori_loop(0, hid // tile, products, 0)
    for i in range(chunks):
        own(i).wait()
        for step in range(1, peers):
            peer = lax.rem(lon + step, peers)
            send(i, peer).wait_send()
            pltpu.make_async_remote_copy(
                src_ref=packed.at[i, pl.ds(peer * cols, cols)],
                dst_ref=moved.at[i, pl.ds(peer * cols, cols)],
                send_sem=send_sem.at[i, peer],
                recv_sem=recv_sem.at[i, peer],
                device_id=(lat, peer),
                device_id_type=MESH,
            ).wait_recv()


def filter_kernel(
    peers, cols, chunks, lat_count, reach, basis_count,
    moved, cot_hbm, forward, inverse, band, cosine, sine, chan,
    out,
    block, cot, wide, turned, packed, landed, up_out, down_out, up_in, down_in,
    load_sem, send_sem, recv_sem, halo_send, halo_recv,
):
    lat, lon = lax.axis_index("lat"), lax.axis_index("lon")
    local = block.shape[2] // ROWS
    total = chunks * ROWS
    stride = band.shape[1]
    freqs = forward.shape[1]
    loads = [pltpu.make_async_copy(moved.at[i], block.at[i], load_sem.at[i]) for i in range(chunks)]
    cot_load = pltpu.make_async_copy(cot_hbm, cot, load_sem.at[chunks])
    for load in loads:
        load.start()
    cot_load.start()
    greet(lat, lon, peers, lat_count)
    zero = jnp.zeros((local, freqs), jnp.float32)
    for r in range(total + 2 * reach, stride):
        for m in range(freqs // LANES):
            wide[m, pl.ds(r, local, stride=stride), :] = zero[:, :LANES]

    def place(values, first, count):
        for r in range(count):
            for m in range(freqs // LANES):
                wide[m, pl.ds(first + r, local, stride=stride), :] = values[
                    r * local : (r + 1) * local, m * LANES : (m + 1) * LANES
                ]

    def halo(source, target, to, at):
        return pltpu.make_async_remote_copy(
            src_ref=source, dst_ref=target, send_sem=halo_send.at[at], recv_sem=halo_recv.at[at],
            device_id=(to, lon), device_id_type=MESH,
        )

    to_prev = halo(up_out, up_in, lat - 1, 0)
    to_next = halo(down_out, down_in, lat + 1, 1)
    order = [0, chunks - 1] + list(range(1, chunks - 1))
    for i in order:
        loads[i].wait()
        spectra = tn(block[i], forward[...])
        place(spectra, reach + i * ROWS, ROWS)
        if i == 0:
            up_out[...] = spectra[: reach * local].astype(jnp.bfloat16)

            @pl.when(lat > 0)
            def _():
                to_prev.start()

        if i == chunks - 1:
            down_out[...] = spectra[(ROWS - reach) * local :].astype(jnp.bfloat16)

            @pl.when(lat < lat_count - 1)
            def _():
                to_next.start()

    @pl.when(lat > 0)
    def _():
        to_next.wait_recv()
        place(down_in[...].astype(jnp.float32), 0, reach)

    @pl.when(lat == 0)
    def _():
        place(jnp.zeros((reach * local, freqs), jnp.float32), 0, reach)

    @pl.when(lat < lat_count - 1)
    def _():
        to_prev.wait_recv()
        place(up_in[...].astype(jnp.float32), reach + total, reach)

    @pl.when(lat == lat_count - 1)
    def _():
        place(jnp.zeros((reach * local, freqs), jnp.float32), reach + total, reach)

    first_chan = lon * local

    def channel(c, carry):
        rows = pl.ds(pl.multiple_of(c * stride, stride), stride)
        lines = jnp.concatenate(
            [wide[m, rows, :].astype(jnp.bfloat16) for m in range(freqs // LANES)], axis=1
        )
        terms = nn(band[...], lines)
        straight = jnp.zeros((total, freqs), jnp.float32)
        crossed = jnp.zeros((total, freqs), jnp.float32)
        for k in range(basis_count):
            gain = chan[k, first_chan + c]
            term = terms[k * total : (k + 1) * total]
            straight = straight + (gain * cosine[k : k + 1, :]) * term
            crossed = crossed + (gain * sine[k : k + 1, :]) * term
        for m in range(freqs // LANES):
            here = straight[:, m * LANES : (m + 1) * LANES]
            if m == freqs // LANES - 1:
                other = pltpu.roll(crossed[:, m * LANES :], LANES // 2, 1)
            else:
                pair = m + 1 - 2 * (m % 2)
                other = crossed[:, pair * LANES : (pair + 1) * LANES]
            turned[m, pl.ds(c, total, stride=local), :] = here + other
        return carry

    lax.fori_loop(0, local, channel, 0)

    def send(i, peer):
        return pltpu.make_async_remote_copy(
            src_ref=packed.at[i, pl.ds(peer * cols, cols)],
            dst_ref=landed.at[i, pl.ds(lon * cols, cols)],
            send_sem=send_sem.at[i, peer],
            recv_sem=recv_sem.at[i, lon],
            device_id=(lat, peer),
            device_id_type=MESH,
        )

    def own(i):
        rows = pl.ds(lon * cols, cols)
        return pltpu.make_async_copy(packed.at[i, rows], landed.at[i, rows], send_sem.at[i, lon])

    for i in range(chunks):
        rows = pl.ds(i * ROWS * local, ROWS * local)
        lines = jnp.concatenate(
            [turned[m, rows, :].astype(jnp.bfloat16) for m in range(freqs // LANES)], axis=1
        )
        packed[i] = nt(inverse[...], lines).astype(jnp.bfloat16)
        for step in range(1, peers):
            send(i, lax.rem(lon + step, peers)).start()
        own(i).start()

    cot_load.wait()
    for i in range(chunks):
        own(i).wait()
        for step in range(1, peers):
            peer = lax.rem(lon + step, peers)
            pltpu.make_async_remote_copy(
                src_ref=packed.at[i, pl.ds(peer * cols, cols)],
                dst_ref=landed.at[i, pl.ds(peer * cols, cols)],
                send_sem=send_sem.at[i, peer],
                recv_sem=recv_sem.at[i, peer],
                device_id=(lat, peer),
                device_id_type=MESH,
            ).wait_recv()
        blocks = [landed[i, s * cols : (s + 1) * cols, :] for s in range(peers)]
        for r, line in enumerate(swap_blocks(blocks, local)):
            at = pl.ds((i * ROWS + r) * cols, cols)
            out[at, :] = (cot[at, :].astype(jnp.float32) + line.astype(jnp.float32)).astype(jnp.bfloat16)
    for i in range(chunks):
        for step in range(1, peers):
            send(i, lax.rem(lon + step, peers)).wait_send()

    @pl.when(lat > 0)
    def _():
        to_prev.wait_send()

    @pl.when(lat < lat_count - 1)
    def _():
        to_next.wait_send()


def split_order(half_len):
    order = []
    whole = half_len // LANES
    for m in range(whole):
        order += list(range(m * LANES, (m + 1) * LANES))
        order += list(range(half_len + m * LANES, half_len + (m + 1) * LANES))
    order += list(range(whole * LANES, half_len)) + list(range(half_len + whole * LANES, 2 * half_len))
    return np.array(order)


def split_lanes(values, half_len):
    whole = half_len // LANES
    pieces = []
    for m in range(whole):
        pieces += [values[:, m * LANES : (m + 1) * LANES], values[:, half_len + m * LANES : half_len + (m + 1) * LANES]]
    pieces += [values[:, whole * LANES : half_len], values[:, half_len + whole * LANES :]]
    return jnp.concatenate(pieces, axis=1)


def lon_tables(lon_total):
    half_len = lon_total // 2
    order = split_order(half_len)
    frequency = order % half_len
    phases = (np.arange(lon_total)[:, None] * frequency[None, :]) % lon_total
    angles = phases * (2.0 * math.pi / lon_total)
    forward = np.where((order >= half_len)[None, :], np.sin(angles), np.cos(angles))
    scaling = np.where(frequency == 0, 1.0, 2.0) / lon_total
    inverse = forward * scaling[None, :]
    return (
        jnp.asarray(forward.astype(np.float32)).astype(jnp.bfloat16),
        jnp.asarray(inverse.astype(np.float32)).astype(jnp.bfloat16),
    )


def fast_body(
    mlp_input, out_cot, w_in, w_out, chan_weights, row_weights, basis_spectra, band_cols, band_widths
):
    lat_rows, lon_cols, channels = mlp_input.shape
    hid = w_in.shape[1]
    peers = lax.axis_size("lon")
    lat_count = lax.axis_size("lat")
    local = channels // peers
    lon_total = lon_cols * peers
    half_len = lon_total // 2
    basis_count, lat_total, slots = row_weights.shape
    reach = (slots - 1) // 2
    chunks = lat_rows // ROWS
    span = ROWS * lon_cols
    tokens = lat_rows * lon_cols
    stride = -(-(lat_rows + 2 * reach) // 16) * 16
    row_start = lax.axis_index("lat") * lat_rows
    any_spec = pl.BlockSpec(memory_space=pl.ANY)
    vmem_spec = pl.BlockSpec(memory_space=pltpu.VMEM)
    smem_spec = pl.BlockSpec(memory_space=pltpu.SMEM)
    bf16, f32 = jnp.bfloat16, jnp.float32
    tok_flat = mlp_input.reshape(tokens, channels)
    cot_flat = out_cot.reshape(tokens, channels)

    with jax.named_scope("mlp"):
        moved, part_in, part_out = pl.pallas_call(
            functools.partial(mlp_kernel, peers, lon_cols, chunks),
            out_shape=(
                jax.ShapeDtypeStruct((chunks, lon_total, ROWS * local), bf16),
                jax.ShapeDtypeStruct((channels, hid), bf16),
                jax.ShapeDtypeStruct((channels, hid), bf16),
            ),
            in_specs=[any_spec] * 4,
            out_specs=(any_spec, vmem_spec, vmem_spec),
            scratch_shapes=[
                pltpu.VMEM((tokens, channels), bf16),
                pltpu.VMEM((tokens, channels), bf16),
                pltpu.VMEM((channels, hid), bf16),
                pltpu.VMEM((hid, channels), bf16),
                pltpu.VMEM((channels, tokens), bf16),
                pltpu.VMEM((channels, tokens), bf16),
                pltpu.VMEM((tokens, hid), bf16),
                pltpu.VMEM((tokens, hid), bf16),
                pltpu.VMEM((chunks, lon_total, ROWS * local), bf16),
                pltpu.SemaphoreType.DMA((2 + 2 * chunks,)),
                pltpu.SemaphoreType.DMA((chunks, peers)),
                pltpu.SemaphoreType.DMA((chunks, peers)),
            ],
            compiler_params=pltpu.CompilerParams(
                collective_id=0, has_side_effects=True, vmem_limit_bytes=48 * 2**20
            ),
            name="mlp_exchange",
        )(tok_flat, cot_flat, w_in, w_out)

    with jax.named_scope("weight_sums"):
        sums_in = lax.psum_scatter(part_in, "lon", scatter_dimension=1, tiled=True)
        sums_out = lax.psum_scatter(part_out, "lon", scatter_dimension=1, tiled=True)
        grad_in = lax.psum_scatter(sums_in.astype(f32), "lat", scatter_dimension=0, tiled=True)
        grad_out = lax.psum_scatter(sums_out.astype(f32), "lat", scatter_dimension=0, tiled=True).T

    with jax.named_scope("band"):
        pad = ((reach, reach),)
        near_cols = lax.dynamic_slice_in_dim(jnp.pad(band_cols, pad + ((0, 0),), constant_values=-1), row_start, lat_rows + 2 * reach, 0)
        near_widths = lax.dynamic_slice_in_dim(jnp.pad(band_widths, pad), row_start, lat_rows + 2 * reach, 0)
        near_weights = lax.dynamic_slice_in_dim(
            jnp.pad(row_weights, ((0, 0),) + pad + ((0, 0),)), row_start, lat_rows + 2 * reach, 1
        )
        targets = row_start + jnp.arange(lat_rows, dtype=jnp.int32)
        band = jnp.zeros((basis_count, lat_rows, lat_rows + 2 * reach), f32)
        for j in range(slots):
            live = (near_cols[None, :, j] == targets[:, None]) & (j < near_widths)[None, :]
            band = band + jnp.where(live[None], near_weights[:, None, :, j], 0.0)
        band = jnp.pad(band, ((0, 0), (0, 0), (0, stride - lat_rows - 2 * reach)))
        band = band.reshape(basis_count * lat_rows, stride).astype(bf16)
        cos_part, sin_part = basis_spectra[:, :half_len], basis_spectra[:, half_len:]
        cosine = split_lanes(jnp.concatenate([cos_part, cos_part], 1), half_len)
        sine = split_lanes(jnp.concatenate([-sin_part, sin_part], 1), half_len)
        forward, inverse = lon_tables(lon_total)

    with jax.named_scope("filter"):
        out = pl.pallas_call(
            functools.partial(filter_kernel, peers, lon_cols, chunks, lat_count, reach, basis_count),
            out_shape=jax.ShapeDtypeStruct((tokens, channels), bf16),
            in_specs=[any_spec, any_spec] + [vmem_spec] * 5 + [smem_spec],
            out_specs=vmem_spec,
            scratch_shapes=[
                pltpu.VMEM((chunks, lon_total, ROWS * local), bf16),
                pltpu.VMEM((tokens, channels), bf16),
                pltpu.VMEM((2 * half_len // LANES, local * stride, LANES), f32),
                pltpu.VMEM((2 * half_len // LANES, local * lat_rows, LANES), f32),
                pltpu.VMEM((chunks, lon_total, ROWS * local), bf16),
                pltpu.VMEM((chunks, lon_total, ROWS * local), bf16),
            ]
            + [pltpu.VMEM((reach * local, 2 * half_len), bf16)] * 4
            + [
                pltpu.SemaphoreType.DMA((chunks + 1,)),
                pltpu.SemaphoreType.DMA((chunks, peers)),
                pltpu.SemaphoreType.DMA((chunks, peers)),
                pltpu.SemaphoreType.DMA((2,)),
                pltpu.SemaphoreType.DMA((2,)),
            ],
            compiler_params=pltpu.CompilerParams(
                collective_id=1, has_side_effects=True, vmem_limit_bytes=48 * 2**20
            ),
            name="filter_exchange",
        )(moved, cot_flat, forward, inverse, band, cosine, sine, chan_weights)
    return (out.reshape(lat_rows, lon_cols, channels), grad_in, grad_out)


def fits(mesh_shape, args):
    lat_count, peers = mesh_shape["lat"], mesh_shape["lon"]
    lat_total, lon_total, channels = args[0].shape
    hid, slots = args[2].shape[1], args[5].shape[2]
    lat_rows, cols, local = lat_total // lat_count, lon_total // peers, channels // peers
    reach = (slots - 1) // 2
    return (
        peers > 1
        and lat_count > 1
        and lat_rows % ROWS == 0
        and lat_rows >= 2 * ROWS
        and reach <= ROWS
        and cols % 16 == 0
        and (ROWS * local) % LANES == 0
        and channels == ROWS * local
        and (ROWS * cols) % LANES == 0
        and (reach * local) % 16 == 0
        and (lon_total // 2) % LANES == LANES // 2
        and hid % 256 == 0
    )


def solution(mesh):
    def run(*args):
        chosen = fast_body if fits(dict(mesh.shape), args) else body
        return jax.shard_map(
            chosen,
            mesh=mesh,
            in_specs=(P("lat", "lon", None), P("lat", "lon", None), P(), P(), P(), P(), P(), P(), P()),
            out_specs=(P("lat", "lon", None), P("lat", "lon"), P("lon", "lat")),
            check_vma=False,
        )(*args)

    return run
```

profile of v0, /device:TPU:1, one launch (start us, length us, event | category | flops | bytes accessed | tf_op | source)
XLA Modules:
  0.0 204.8 jit_solution(8659695619741863903)
XLA Ops:
  7.2 0.0 reduce-scatter.15.cloned.1.call-start
  7.2 0.0 copy-start.1
  7.2 1.4 copy-done.1
  8.6 31.1 %mlp_exchange.1 = (bf16[4,384,640]{2,1,0:T(8,128)(2,1)}, bf16[640,1280]{1,0:T(8,128)(2,1)S(1)}, bf16[640,1280]{1,0:T(8,128)(2,1)S(1)}) custom-call(bf16[1536,640]{1,0:T(8,128)(2,1)} %bitcast.51, bf16[1536,640]{1,0:T(8,128)(2,1)} %bitcast.47, bf16[640,1280]{1,0:T(8,128)(2,1)S(1)} %copy-done.1, bf16[1280,640]{1,0:T(8,128)(2,1)} %wout_hbm.1), custom_call_target="tpu_custom_call" | custom-call | tf_op jit(solution)/shard_map/mlp/mlp_exchange/pallas_call | solution.py:518
  39.8 2.2 %copy.21 = bf16[640,1280]{0,1:T(8,128)(2,1)} copy(bf16[640,1280]{1,0:T(8,128)(2,1)S(1)} %get-tuple-element.8) | data formatting | bytes 3276800
  42.0 0.0 reduce-scatter.15.cloned.1.call-update
  42.0 0.0 reduce-scatter.13.cloned.1.call-start
  42.0 2.2 %copy.19 = bf16[640,1280]{0,1:T(8,128)(2,1)} copy(bf16[640,1280]{1,0:T(8,128)(2,1)S(1)} %get-tuple-element.7) | data formatting | bytes 3276800
  44.2 0.0 copy-start.8
  44.2 0.0 copy-start.6
  44.2 0.0 copy-start.7
  44.3 0.0 reduce-scatter.13.cloned.1.call-update
  44.3 0.0 copy-start.5
  44.3 0.0 reduce-scatter.11.cloned.1.call-start
  44.3 0.6 copy-done.8
  44.9 0.1 broadcast_compare_fusion.8
  45.0 36.5 %reduce-scatter.15.cloned.1.call-done = bf16[160,640]{1,0:T(8,128)(2,1)} async-done(((bf16[1280,640]{1,0:T(8,128)(2,1)}), bf16[160,640]{1,0:T(8,128)(2,1)}) %reduce-scatter.15.cloned.1.call-update) | async-done | bytes 204816
  81.5 1.1 copy.22
  82.6 0.9 convert_element_type.23
  83.5 0.0 reduce-scatter.11.cloned.1.call-update
  83.5 0.2 reduce-scatter.9.cloned.1.call-start
  83.7 0.0 copy-start.2
  83.8 0.0 copy-start.3
  83.8 0.0 copy-start.4
  83.8 0.0 copy-done.6
  83.8 0.0 copy-done.7
  83.8 0.1 fusion.9
  83.9 0.1 compare_and_fusion.8
  84.1 0.0 copy-done.5
  84.1 0.1 slice_negate_fusion
  84.1 40.0 %reduce-scatter.13.cloned.1.call-done = bf16[160,640]{1,0:T(8,128)(2,1)} async-done(((bf16[1280,640]{1,0:T(8,128)(2,1)}), bf16[160,640]{1,0:T(8,128)(2,1)}) %reduce-scatter.13.cloned.1.call-update) | async-done | bytes 204816
  124.2 1.1 copy.20
  125.3 0.9 convert_element_type.22
  126.2 0.0 reduce-scatter.9.cloned.1.call-update
  126.2 0.1 fusion
  126.3 0.1 add_convert_fusion
  126.5 0.1 fusion.19
  126.6 0.1 fusion.18
  126.6 0.1 pad_maximum_fusion
  126.7 0.0 copy-done.2
  126.7 0.0 copy-done.3
  126.7 0.0 copy-done.4
  126.7 0.0 copy-start
  126.7 1.5 copy-done
  128.3 67.0 %filter_exchange.1 = bf16[1536,640]{1,0:T(8,128)(2,1)S(1)} custom-call(bf16[4,384,640]{2,1,0:T(8,128)(2,1)S(1)} %copy-done, bf16[1536,640]{1,0:T(8,128)(2,1)} %bitcast.48, bf16[384,384]{1,0:T(8,128)(2,1)S(1)} %copy-done.3, bf16[384,384]{1,0:T(8,128)(2,1)S(1)} %copy-done.2, bf16[288,48]{1,0:T(8,128)(2,1)S(1)} %bitcast.46, ...), custom_call_target="tpu_custom_call" | custom-call | tf_op jit(solution)/shard_map/filter/filter_exchange/pallas_call | solution.py:573
  195.3 0.0 reduce-scatter.11.cloned.1.call-done
  195.3 1.7 copy.18
  197.0 0.0 reduce-scatter.9.cloned.1.call-done
  197.0 1.3 copy.24
  (6 shorter events, 0.1 us)
Async XLA Ops:
  7.2 74.3 %reduce-scatter.15.cloned.1.call-start = ((), (), s32[]{:S(2)}) async-start(), calls=%async_computation.7 | async-start | bytes 1843200
  7.2 1.4 copy-start.1
  42.0 82.2 %reduce-scatter.13.cloned.1.call-start = ((), (), s32[]{:S(2)}) async-start(), calls=%async_computation.6 | async-start | bytes 1843200
  44.2 0.7 copy-start.8
  44.2 39.5 %copy-start.6 = (f32[9,128,9]{1,2,0:T(8,128)S(1)}, f32[9,128,9]{1,2,0:T(8,128)}, u32[]{:S(2)}) copy-start(f32[9,128,9]{1,2,0:T(8,128)} %param.16) | copy-start | bytes 124420
  44.2 39.6 %copy-start.7 = (s32[128,9]{0,1:T(8,128)S(1)}, s32[128,9]{0,1:T(8,128)}, u32[]{:S(2)}) copy-start(s32[128,9]{0,1:T(8,128)} %param.18) | copy-start | bytes 13828
  44.3 39.8 %copy-start.5 = (f32[9,384]{1,0:T(8,128)S(1)}, f32[9,384]{1,0:T(8,128)}, u32[]{:S(2)}) copy-start(f32[9,384]{1,0:T(8,128)} %param.17) | copy-start | bytes 41476
  44.3 151.0 %reduce-scatter.11.cloned.1.call-start = ((), (), s32[]{:S(2)}) async-start(), calls=%async_computation.5 | async-start | bytes 819200 | tf_op jit(solution)/shard_map/weight_sums/reduce_scatter | solution.py:551
  83.5 113.5 %reduce-scatter.9.cloned.1.call-start = ((), (), s32[]{:S(2)}) async-start(), calls=%async_computation.4 | async-start | bytes 819200 | tf_op jit(solution)/shard_map/weight_sums/reduce_scatter | solution.py:550
  83.7 43.0 %copy-start.2 = (bf16[384,384]{1,0:T(8,128)(2,1)S(1)}, bf16[384,384]{1,0:T(8,128)(2,1)}, u32[]{:S(2)}) copy-start(bf16[384,384]{1,0:T(8,128)(2,1)} %constant.50.inverse) | copy-start | bytes 884740
  83.8 43.0 %copy-start.3 = (bf16[384,384]{1,0:T(8,128)(2,1)S(1)}, bf16[384,384]{1,0:T(8,128)(2,1)}, u32[]{:S(2)}) copy-start(bf16[384,384]{1,0:T(8,128)(2,1)} %constant.49.forward) | copy-start | bytes 884740
  83.8 42.9 %copy-start.4 = (f32[9,640]{1,0:T(8,128)S(1)}, f32[9,640]{1,0:T(8,128)}, u32[]{:S(2)}) copy-start(f32[9,640]{1,0:T(8,128)} %chan.1) | copy-start | bytes 69124
  126.7 1.5 copy-start
Sparse Core Ops, SparseCore 0:
  42.1 39.3 reduce-scatter.14
  85.4 38.7 reduce-scatter.12
  126.5 25.8 reduce-scatter.10
  155.1 20.3 reduce-scatter.8
where the time goes:
time: 205 us
  Pallas kernels  98.1 us (48%)
  waiting for transfers between devices  76.6 us (37%)
  between operations  14 us (7%)
  local copies, waits for them, and re-layouts  13.5 us (7%)
  other arithmetic  2.24 us (1%)
    unnamed x6, waiting for transfers between devices  76.6 us
    pallas_call x1, Pallas kernels, fast_body(): pl.pallas_call(functools.partial(filter_kernel, peers, lon_cols, chunks,...  67 us
    pallas_call x1, Pallas kernels, fast_body(): pl.pallas_call(functools.partial(mlp_kernel, peers, lon_cols, chunks), ou...  31.1 us
    unnamed x25, local copies, waits for them, and re-layouts  13.1 us
  transfers between devices with their start and end apart: 4, of which 2 were waited for; matrix products, arithmetic and copies ran while one was open for 4% of the time, Pallas kernels for 33%

commit v1 on v0

--- a/solution.py
+++ b/solution.py
@@ -172,6 +172,7 @@
 
 MESH = pl.DeviceIdType.MESH
 ROWS = 8
+GROUPS = 2
 LANES = 128
 SLOPE = 0.7978845608
 
@@ -203,18 +204,19 @@
             barrier, inc=1, device_id=(lat, lax.rem(lon + step, peers)), device_id_type=MESH
         )
     if lat_count:
-        for step in (1, lat_count - 1):
+        for step in range(1, lat_count):
             pl.semaphore_signal(
                 barrier, inc=1, device_id=(lax.rem(lat + step, lat_count), lon), device_id_type=MESH
             )
-    pl.semaphore_wait(barrier, peers + 1 if lat_count else peers - 1)
+    pl.semaphore_wait(barrier, peers - 1 + max(lat_count - 1, 0))
 
 
 def mlp_kernel(
     peers, cols, chunks,
     tok_hbm, cot_hbm, win_hbm, wout_hbm,
-    moved, part_in, part_out,
-    tok, cot, win, wout, tok_t, cot_t, hidden, grad, packed, load_sem, send_sem, recv_sem,
+    moved, half,
+    tok, cot, win, wout, tok_t, cot_t, hidden, grad, packed, parts, pair_in,
+    load_sem, send_sem, recv_sem, pair_send, pair_recv,
 ):
     lat, lon = lax.axis_index("lat"), lax.axis_index("lon")
     span = ROWS * cols
@@ -275,16 +277,40 @@
         for step in range(1, peers):
             send(i, lax.rem(lon + step, peers)).start()
         own(i).start()
-        tok_t[:, i * span : (i + 1) * span] = here.T
-        cot_t[:, i * span : (i + 1) * span] = cotan.T
+
+    for i in range(chunks):
+        tok_t[:, i * span : (i + 1) * span] = tok[i * span : (i + 1) * span, :].T
+        cot_t[:, i * span : (i + 1) * span] = cot[i * span : (i + 1) * span, :].T
 
     def products(j, carry):
         at = pl.ds(pl.multiple_of(j * tile, tile), tile)
-        part_in[:, at] = nn(tok_t[...], grad[:, at]).astype(jnp.bfloat16)
-        part_out[:, at] = nn(cot_t[...], hidden[:, at]).astype(jnp.bfloat16)
+        parts[0, at, :] = nn(tok_t[...], grad[:, at]).T.astype(jnp.bfloat16)
+        parts[1, at, :] = nn(cot_t[...], hidden[:, at]).T.astype(jnp.bfloat16)
         return carry
 
     lax.fori_loop(0, hid // tile, products, 0)
+    piece = hid // peers
+    core = lax.rem(lon, 2)
+
+    def to_pair(kind, q):
+        return pltpu.make_async_remote_copy(
+            src_ref=parts.at[kind, pl.ds((2 * q + 1 - core) * piece, piece)],
+            dst_ref=pair_in.at[q, kind],
+            send_sem=pair_send.at[q, kind],
+            recv_sem=pair_recv.at[q, kind],
+            device_id=(lat, lon + 1 - 2 * core),
+            device_id_type=MESH,
+        )
+
+    for q in range(peers // 2):
+        for kind in range(2):
+            to_pair(kind, q).start()
+    for q in range(peers // 2):
+        for kind in range(2):
+            to_pair(kind, q).wait()
+            mine = parts[kind, pl.ds(pl.multiple_of((2 * q + core) * piece, 16), piece), :]
+            both = mine.astype(jnp.float32) + pair_in[q, kind].astype(jnp.float32)
+            half[q, kind] = both.astype(jnp.bfloat16)
     for i in range(chunks):
         own(i).wait()
         for step in range(1, peers):
@@ -302,10 +328,12 @@
 
 def filter_kernel(
     peers, cols, chunks, lat_count, reach, basis_count,
-    moved, cot_hbm, forward, inverse, band, cosine, sine, chan,
-    out,
+    moved, cot_hbm, half, forward, inverse, band, cosine, sine, chan,
+    out, grad_in, grad_out,
     block, cot, wide, turned, packed, landed, up_out, down_out, up_in, down_in,
+    lon_in, lat_out, lat_in,
     load_sem, send_sem, recv_sem, halo_send, halo_recv,
+    lon_send, lon_recv, lat_send, lat_recv,
 ):
     lat, lon = lax.axis_index("lat"), lax.axis_index("lon")
     local = block.shape[2] // ROWS
@@ -318,6 +346,42 @@
         load.start()
     cot_load.start()
     greet(lat, lon, peers, lat_count)
+    chips = peers // 2
+    chip, core = lax.div(lon, 2), lax.rem(lon, 2)
+
+    def to_chip(other):
+        return pltpu.make_async_remote_copy(
+            src_ref=half.at[other], dst_ref=lon_in.at[chip],
+            send_sem=lon_send.at[other], recv_sem=lon_recv.at[chip],
+            device_id=(lat, 2 * other + core), device_id_type=MESH,
+        )
+
+    def from_chip(other):
+        return pltpu.make_async_remote_copy(
+            src_ref=half.at[other], dst_ref=lon_in.at[other],
+            send_sem=lon_send.at[other], recv_sem=lon_recv.at[other],
+            device_id=(lat, 2 * other + core), device_id_type=MESH,
+        )
+
+    def to_lat(other):
+        return pltpu.make_async_remote_copy(
+            src_ref=lat_out.at[other], dst_ref=lat_in.at[lat],
+            send_sem=lat_send.at[other], recv_sem=lat_recv.at[lat],
+            device_id=(other, lon), device_id_type=MESH,
+        )
+
+    def from_lat(other):
+        return pltpu.make_async_remote_copy(
+            src_ref=lat_out.at[other], dst_ref=lat_in.at[other],
+            send_sem=lat_send.at[other], recv_sem=lat_recv.at[other],
+            device_id=(other, lon), device_id_type=MESH,
+        )
+
+    chip_own = pltpu.make_async_copy(half.at[chip], lon_in.at[chip], lon_send.at[chip])
+    lat_own = pltpu.make_async_copy(lat_out.at[lat], lat_in.at[lat], lat_send.at[lat])
+    chip_own.start()
+    for step in range(1, chips):
+        to_chip(lax.rem(chip + step, chips)).start()
     zero = jnp.zeros((local, freqs), jnp.float32)
     for r in range(total + 2 * reach, stride):
         for m in range(freqs // LANES):
@@ -376,31 +440,8 @@
         place(jnp.zeros((reach * local, freqs), jnp.float32), reach + total, reach)
 
     first_chan = lon * local
-
-    def channel(c, carry):
-        rows = pl.ds(pl.multiple_of(c * stride, stride), stride)
-        lines = jnp.concatenate(
-            [wide[m, rows, :].astype(jnp.bfloat16) for m in range(freqs // LANES)], axis=1
-        )
-        terms = nn(band[...], lines)
-        straight = jnp.zeros((total, freqs), jnp.float32)
-        crossed = jnp.zeros((total, freqs), jnp.float32)
-        for k in range(basis_count):
-            gain = chan[k, first_chan + c]
-            term = terms[k * total : (k + 1) * total]
-            straight = straight + (gain * cosine[k : k + 1, :]) * term
-            crossed = crossed + (gain * sine[k : k + 1, :]) * term
-        for m in range(freqs // LANES):
-            here = straight[:, m * LANES : (m + 1) * LANES]
-            if m == freqs // LANES - 1:
-                other = pltpu.roll(crossed[:, m * LANES :], LANES // 2, 1)
-            else:
-                pair = m + 1 - 2 * (m % 2)
-                other = crossed[:, pair * LANES : (pair + 1) * LANES]
-            turned[m, pl.ds(c, total, stride=local), :] = here + other
-        return carry
-
-    lax.fori_loop(0, local, channel, 0)
+    part = local // GROUPS
+    together = 4
 
     def send(i, peer):
         return pltpu.make_async_remote_copy(
@@ -416,16 +457,74 @@
         rows = pl.ds(lon * cols, cols)
         return pltpu.make_async_copy(packed.at[i, rows], landed.at[i, rows], send_sem.at[i, lon])
 
-    for i in range(chunks):
-        rows = pl.ds(i * ROWS * local, ROWS * local)
-        lines = jnp.concatenate(
-            [turned[m, rows, :].astype(jnp.bfloat16) for m in range(freqs // LANES)], axis=1
-        )
-        packed[i] = nt(inverse[...], lines).astype(jnp.bfloat16)
-        for step in range(1, peers):
-            send(i, lax.rem(lon + step, peers)).start()
-        own(i).start()
-
+    tiles = freqs // LANES
+    for group in range(GROUPS):
+
+        def channels(step, carry):
+            for u in range(together):
+                inner = step * together + u
+                c = group * part + inner
+                rows = pl.ds(pl.multiple_of(c * stride, stride), stride)
+                lines = jnp.concatenate(
+                    [wide[m, rows, :].astype(jnp.bfloat16) for m in range(tiles)], axis=1
+                )
+                terms = nn(band[...], lines).reshape(basis_count, total // 8, 8, freqs)
+                straight = crossed = None
+                for k in range(basis_count):
+                    gain = chan[k, first_chan + c]
+                    one = (gain * cosine[k])[None] * terms[k]
+                    two = (gain * sine[k])[None] * terms[k]
+                    straight = one if k == 0 else straight + one
+                    crossed = two if k == 0 else crossed + two
+                straight = straight.reshape(total, freqs)
+                crossed = crossed.reshape(total, freqs)
+                for m in range(tiles):
+                    here = straight[:, m * LANES : (m + 1) * LANES]
+                    if m == tiles - 1:
+                        other = pltpu.roll(crossed[:, m * LANES :], LANES // 2, 1)
+                    else:
+                        pair = m + 1 - 2 * (m % 2)
+                        other = crossed[:, pair * LANES : (pair + 1) * LANES]
+                    turned[m, pl.ds(group * part * total + inner, total, stride=part), :] = here + other
+            return carry
+
+        lax.fori_loop(0, part // together, channels, 0)
+        for i in range(group * chunks // GROUPS, (group + 1) * chunks // GROUPS):
+            rows = pl.ds(i * ROWS * local, ROWS * local)
+            lines = jnp.concatenate(
+                [turned[m, rows, :].astype(jnp.bfloat16) for m in range(tiles)], axis=1
+            )
+            packed[i] = nt(inverse[...], lines).astype(jnp.bfloat16)
+            for step in range(1, peers):
+                send(i, lax.rem(lon + step, peers)).start()
+            own(i).start()
+        if group == 0:
+            chip_own.wait()
+            for step in range(1, chips):
+                from_chip(lax.rem(chip + step, chips)).wait_recv()
+            share = lat_out.shape[2]
+            for kind in range(2):
+                summed = lon_in[0, kind].astype(jnp.float32)
+                for q in range(1, chips):
+                    summed = summed + lon_in[q, kind].astype(jnp.float32)
+                summed = summed.T.astype(jnp.bfloat16)
+                for z in range(lat_count):
+                    lat_out[z, kind] = summed[z * share : (z + 1) * share]
+            lat_own.start()
+            for step in range(1, lat_count):
+                to_lat(lax.rem(lat + step, lat_count)).start()
+
+    lat_own.wait()
+    for step in range(1, lat_count):
+        from_lat(lax.rem(lat + step, lat_count)).wait_recv()
+    sums = []
+    for kind in range(2):
+        summed = lat_in[0, kind].astype(jnp.float32)
+        for z in range(1, lat_count):
+            summed = summed + lat_in[z, kind].astype(jnp.float32)
+        sums.append(summed)
+    grad_in[...] = sums[0]
+    grad_out[...] = sums[1].T
     cot_load.wait()
     for i in range(chunks):
         own(i).wait()
@@ -439,13 +538,24 @@
                 device_id=(lat, peer),
                 device_id_type=MESH,
             ).wait_recv()
-        blocks = [landed[i, s * cols : (s + 1) * cols, :] for s in range(peers)]
-        for r, line in enumerate(swap_blocks(blocks, local)):
-            at = pl.ds((i * ROWS + r) * cols, cols)
-            out[at, :] = (cot[at, :].astype(jnp.float32) + line.astype(jnp.float32)).astype(jnp.bfloat16)
+        held = chunks // GROUPS
+        if i >= chunks - held:
+            late = i - (chunks - held)
+            blocks = [
+                landed[group * held + late, s * cols : (s + 1) * cols, :]
+                for s in range(peers)
+                for group in range(GROUPS)
+            ]
+            for r, line in enumerate(swap_blocks(blocks, part)):
+                at = pl.ds((late * ROWS * GROUPS + r) * cols, cols)
+                out[at, :] = (cot[at, :].astype(jnp.float32) + line.astype(jnp.float32)).astype(jnp.bfloat16)
     for i in range(chunks):
         for step in range(1, peers):
             send(i, lax.rem(lon + step, peers)).wait_send()
+    for step in range(1, chips):
+        to_chip(lax.rem(chip + step, chips)).wait_send()
+    for step in range(1, lat_count):
+        to_lat(lax.rem(lat + step, lat_count)).wait_send()
 
     @pl.when(lat > 0)
     def _():
@@ -515,15 +625,14 @@
     cot_flat = out_cot.reshape(tokens, channels)
 
     with jax.named_scope("mlp"):
-        moved, part_in, part_out = pl.pallas_call(
+        moved, half = pl.pallas_call(
             functools.partial(mlp_kernel, peers, lon_cols, chunks),
             out_shape=(
                 jax.ShapeDtypeStruct((chunks, lon_total, ROWS * local), bf16),
-                jax.ShapeDtypeStruct((channels, hid), bf16),
-                jax.ShapeDtypeStruct((channels, hid), bf16),
+                jax.ShapeDtypeStruct((peers // 2, 2, hid // peers, channels), bf16),
             ),
             in_specs=[any_spec] * 4,
-            out_specs=(any_spec, vmem_spec, vmem_spec),
+            out_specs=(any_spec, vmem_spec),
             scratch_shapes=[
                 pltpu.VMEM((tokens, channels), bf16),
                 pltpu.VMEM((tokens, channels), bf16),
@@ -534,21 +643,19 @@
                 pltpu.VMEM((tokens, hid), bf16),
                 pltpu.VMEM((tokens, hid), bf16),
                 pltpu.VMEM((chunks, lon_total, ROWS * local), bf16),
+                pltpu.VMEM((2, hid, channels), bf16),
+                pltpu.VMEM((peers // 2, 2, hid // peers, channels), bf16),
                 pltpu.SemaphoreType.DMA((2 + 2 * chunks,)),
                 pltpu.SemaphoreType.DMA((chunks, peers)),
                 pltpu.SemaphoreType.DMA((chunks, peers)),
+                pltpu.SemaphoreType.DMA((peers // 2, 2)),
+                pltpu.SemaphoreType.DMA((peers // 2, 2)),
             ],
             compiler_params=pltpu.CompilerParams(
                 collective_id=0, has_side_effects=True, vmem_limit_bytes=48 * 2**20
             ),
             name="mlp_exchange",
         )(tok_flat, cot_flat, w_in, w_out)
-
-    with jax.named_scope("weight_sums"):
-        sums_in = lax.psum_scatter(part_in, "lon", scatter_dimension=1, tiled=True)
-        sums_out = lax.psum_scatter(part_out, "lon", scatter_dimension=1, tiled=True)
-        grad_in = lax.psum_scatter(sums_in.astype(f32), "lat", scatter_dimension=0, tiled=True)
-        grad_out = lax.psum_scatter(sums_out.astype(f32), "lat", scatter_dimension=0, tiled=True).T
 
     with jax.named_scope("band"):
         pad = ((reach, reach),)
@@ -567,14 +674,20 @@
         cos_part, sin_part = basis_spectra[:, :half_len], basis_spectra[:, half_len:]
         cosine = split_lanes(jnp.concatenate([cos_part, cos_part], 1), half_len)
         sine = split_lanes(jnp.concatenate([-sin_part, sin_part], 1), half_len)
+        cosine = jnp.broadcast_to(cosine[:, None, :], (basis_count, 8, 2 * half_len))
+        sine = jnp.broadcast_to(sine[:, None, :], (basis_count, 8, 2 * half_len))
         forward, inverse = lon_tables(lon_total)
 
     with jax.named_scope("filter"):
-        out = pl.pallas_call(
+        out, grad_in, grad_out = pl.pallas_call(
             functools.partial(filter_kernel, peers, lon_cols, chunks, lat_count, reach, basis_count),
-            out_shape=jax.ShapeDtypeStruct((tokens, channels), bf16),
-            in_specs=[any_spec, any_spec] + [vmem_spec] * 5 + [smem_spec],
-            out_specs=vmem_spec,
+            out_shape=(
+                jax.ShapeDtypeStruct((tokens, channels), bf16),
+                jax.ShapeDtypeStruct((channels // lat_count, hid // peers), f32),
+                jax.ShapeDtypeStruct((hid // peers, channels // lat_count), f32),
+            ),
+            in_specs=[any_spec] * 3 + [vmem_spec] * 5 + [smem_spec],
+            out_specs=(vmem_spec,) * 3,
             scratch_shapes=[
                 pltpu.VMEM((chunks, lon_total, ROWS * local), bf16),
                 pltpu.VMEM((tokens, channels), bf16),
@@ -584,18 +697,24 @@
                 pltpu.VMEM((chunks, lon_total, ROWS * local), bf16),
             ]
             + [pltpu.VMEM((reach * local, 2 * half_len), bf16)] * 4
+            + [pltpu.VMEM((peers // 2, 2, hid // peers, channels), bf16)]
+            + [pltpu.VMEM((lat_count, 2, channels // lat_count, hid // peers), bf16)] * 2
             + [
                 pltpu.SemaphoreType.DMA((chunks + 1,)),
                 pltpu.SemaphoreType.DMA((chunks, peers)),
                 pltpu.SemaphoreType.DMA((chunks, peers)),
                 pltpu.SemaphoreType.DMA((2,)),
                 pltpu.SemaphoreType.DMA((2,)),
+                pltpu.SemaphoreType.DMA((peers // 2,)),
+                pltpu.SemaphoreType.DMA((peers // 2,)),
+                pltpu.SemaphoreType.DMA((lat_count,)),
+                pltpu.SemaphoreType.DMA((lat_count,)),
             ],
             compiler_params=pltpu.CompilerParams(
                 collective_id=1, has_side_effects=True, vmem_limit_bytes=48 * 2**20
             ),
             name="filter_exchange",
-        )(moved, cot_flat, forward, inverse, band, cosine, sine, chan_weights)
+        )(moved, cot_flat, half, forward, inverse, band, cosine, sine, chan_weights)
     return (out.reshape(lat_rows, lon_cols, channels), grad_in, grad_out)
 
 
@@ -606,8 +725,14 @@
     lat_rows, cols, local = lat_total // lat_count, lon_total // peers, channels // peers
     reach = (slots - 1) // 2
     return (
-        peers > 1
+        peers > 2
+        and peers % 2 == 0
         and lat_count > 1
+        and (lat_rows // ROWS) % GROUPS == 0
+        and local % (4 * GROUPS) == 0
+        and (hid // peers) % 16 == 0
+        and channels % (16 * lat_count) == 0
+        and lat_rows % 8 == 0
         and lat_rows % ROWS == 0
         and lat_rows >= 2 * ROWS
         and reach <= ROWS

time: 205 us -> 91.3 us (0.45)
  waiting for transfers between devices: 76.6 us -> 0 us
  Pallas kernels: 98.1 us -> 79 us
  between operations: 14 us -> 0.75 us
  local copies, waits for them, and re-layouts: 13.5 us -> 9.2 us
    unnamed x6 -> x0, waiting for transfers between devices: 76.6 us -> none
    pallas_call x1, Pallas kernels: 67 us -> 47.1 us  [fast_body(): pl.pallas_call(functools.partial(filter_kernel, peers, lon_cols, chunks,...]
    unnamed x25 -> x14, local copies, waits for them, and re-layouts: 13.1 us -> 6.37 us
  transfers between devices with their start and end apart: 4 -> 0, of which waited for: 2 -> 0; matrix products, arithmetic and copies ran while one was open for 4% -> 0% of each run, Pallas kernels for 33% -> 0%
where the time goes in v1:
time: 91.3 us; the launch traced here: 90.9 us
  Pallas kernels  79 us (87%)
  local copies, waits for them, and re-layouts  9.2 us (10%)
  other arithmetic  1.91 us (2%)
    pallas_call x1, Pallas kernels, fast_body(): pl.pallas_call(functools.partial(filter_kernel, peers, lon_cols, chunks,...  47.1 us
    pallas_call x1, Pallas kernels, fast_body(): pl.pallas_call(functools.partial(mlp_kernel, peers, lon_cols, chunks), ou...  31.9 us
    unnamed x14, local copies, waits for them, and re-layouts  6.37 us

profile of v1, /device:TPU:1, one launch (start us, length us, event | category | flops | bytes accessed | tf_op | source)
XLA Modules:
  0.0 90.9 jit_solution(12420264716424224205)
XLA Ops:
  0.6 0.7 broadcast_compare_fusion.8
  1.4 1.1 %fusion.9 = (s32[40]{0:T(128)S(1)}, s32[40]{0:T(128)S(1)}, s32[40]{0:T(128)S(1)}, s32[40]{0:T(128)S(1)}, s32[40]{0:T(128)S(1)}, /*index=5*/s32[40]{0:T(128)S(1)}, s32[40]{0:T(128)S(1)}, s32[40]{0:T(128)S(1)}, s32[40]{0:T(128)S(1)}) fusion(s32[]{:T(128)S(6)} %select_n.33, s32[128,9]{0,1:T(8,128)} %param.18, s32[]{:T(128)S(6)} %add.70, s32[]{:T(128)S(6)} %add.68, ...), kind=kLoop, calls=%fused_computation.42 | loop fusion | bytes 6084 | tf_op jit(solution)/shard_map/band/eq | solution.py:670
  2.5 0.8 fusion.19
  3.3 0.8 fusion.18
  4.1 0.1 compare_and_fusion.8
  4.2 0.9 slice_negate_fusion
  5.1 0.1 pad_maximum_fusion
  5.1 0.9 copy.14
  6.0 0.1 fusion
  6.2 0.1 add_convert_fusion
  6.3 0.0 copy-start
  6.3 1.4 %copy-done = bf16[640,1280]{1,0:T(8,128)(2,1)S(1)} copy-done((bf16[640,1280]{1,0:T(8,128)(2,1)S(1)}, bf16[640,1280]{1,0:T(8,128)(2,1)}, u32[]{:S(2)}) %copy-start) | copy-done | bytes 1638424
  7.8 0.0 copy-start.1
  7.8 1.4 %copy-done.1 = bf16[1280,640]{1,0:T(8,128)(2,1)S(1)} copy-done((bf16[1280,640]{1,0:T(8,128)(2,1)S(1)}, bf16[1280,640]{1,0:T(8,128)(2,1)}, u32[]{:S(2)}) %copy-start.1) | copy-done | bytes 1638424
  9.2 0.0 copy-start.2
  9.2 0.0 copy-start.3
  9.2 0.0 copy-start.4
  9.2 31.9 %mlp_exchange.1 = (bf16[4,384,640]{2,1,0:T(8,128)(2,1)}, bf16[4,2,160,640]{3,2,1,0:T(8,128)(2,1)S(1)}) custom-call(bf16[1536,640]{1,0:T(8,128)(2,1)} %bitcast.44, bf16[1536,640]{1,0:T(8,128)(2,1)} %bitcast.42, bf16[640,1280]{1,0:T(8,128)(2,1)S(1)} %copy-done, bf16[1280,640]{1,0:T(8,128)(2,1)S(1)} %copy-done.1), custom_call_target="tpu_custom_call" | custom-call | tf_op jit(solution)/shard_map/mlp/mlp_exchange/pallas_call | solution.py:628
  41.1 0.0 copy-done.2
  41.2 0.0 copy-done.3
  41.2 0.0 copy-done.4
  41.2 47.1 %filter_exchange.1 = (bf16[1536,640]{1,0:T(8,128)(2,1)S(1)}, f32[160,160]{1,0:T(8,128)S(1)}, f32[160,160]{1,0:T(8,128)S(1)}) custom-call(bf16[4,384,640]{2,1,0:T(8,128)(2,1)} %get-tuple-element.8.moved, bf16[1536,640]{1,0:T(8,128)(2,1)} %bitcast.43, bf16[4,2,160,640]{3,2,1,0:T(8,128)(2,1)S(1)} %get-tuple-element.9.half, bf16[384,384]{1,0:T(8,128)(2,1)S(1)} %copy-done.3, ...), custom_call_target="tpu_custom_call" | custom-call | tf_op jit(solution)/shard_map/filter/filter_exchange/pallas_call | solution.py:682
  88.3 1.3 %copy.18 = bf16[32,48,640]{2,1,0:T(8,128)(2,1)} copy(bf16[32,48,640]{2,1,0:T(8,128)(2,1)S(1)} %bitcast.40) | data formatting | bytes 3932160
  89.5 0.7 copy.19
  90.2 0.7 copy.20
  (7 shorter events, 0.1 us)
Async XLA Ops:
  6.3 1.4 %copy-start = (bf16[640,1280]{1,0:T(8,128)(2,1)S(1)}, bf16[640,1280]{1,0:T(8,128)(2,1)}, u32[]{:S(2)}) copy-start(bf16[640,1280]{1,0:T(8,128)(2,1)} %win_hbm.1) | copy-start | bytes 4915204
  7.8 1.4 %copy-start.1 = (bf16[1280,640]{1,0:T(8,128)(2,1)S(1)}, bf16[1280,640]{1,0:T(8,128)(2,1)}, u32[]{:S(2)}) copy-start(bf16[1280,640]{1,0:T(8,128)(2,1)} %wout_hbm.1) | copy-start | bytes 4915204
  9.2 31.9 %copy-start.2 = (bf16[384,384]{1,0:T(8,128)(2,1)S(1)}, bf16[384,384]{1,0:T(8,128)(2,1)}, u32[]{:S(2)}) copy-start(bf16[384,384]{1,0:T(8,128)(2,1)} %constant.50.inverse) | copy-start | bytes 884740
  9.2 32.0 %copy-start.3 = (bf16[384,384]{1,0:T(8,128)(2,1)S(1)}, bf16[384,384]{1,0:T(8,128)(2,1)}, u32[]{:S(2)}) copy-start(bf16[384,384]{1,0:T(8,128)(2,1)} %constant.49.forward) | copy-start | bytes 884740
  9.2 32.0 %copy-start.4 = (f32[9,640]{1,0:T(8,128)S(1)}, f32[9,640]{1,0:T(8,128)}, u32[]{:S(2)}) copy-start(f32[9,640]{1,0:T(8,128)} %chan.1) | copy-start | bytes 69124

commit v2 on v1

--- a/solution.py
+++ b/solution.py
@@ -173,6 +173,7 @@
 MESH = pl.DeviceIdType.MESH
 ROWS = 8
 GROUPS = 2
+VMEM_BYTES = 62 * 2**20
 LANES = 128
 SLOPE = 0.7978845608
 
@@ -211,53 +212,97 @@
     pl.semaphore_wait(barrier, peers - 1 + max(lat_count - 1, 0))
 
 
-def mlp_kernel(
-    peers, cols, chunks,
-    tok_hbm, cot_hbm, win_hbm, wout_hbm,
-    moved, half,
-    tok, cot, win, wout, tok_t, cot_t, hidden, grad, packed, parts, pair_in,
-    load_sem, send_sem, recv_sem, pair_send, pair_recv,
+def exchange_kernel(
+    peers, cols, chunks, lat_count, reach, basis_count,
+    tok_hbm, cot_hbm, win_hbm, wout_hbm, table_hbm, weights, near, widths, spectrum, chan,
+    out, grad_in, grad_out,
+    tok, cot, win, wout, tok_t, cot_t, hidden, grad, moving, block, parts, pair_in, half,
+    band, cosine, sine, table, forward, inverse,
+    wide, turned, packed, landed, up_out, down_out, up_in, down_in,
+    lon_in, lat_out, lat_in,
+    load_sem, to_sem, from_sem, pair_send, pair_recv,
+    send_sem, recv_sem, halo_send, halo_recv,
+    lon_send, lon_recv, lat_send, lat_recv,
 ):
     lat, lon = lax.axis_index("lat"), lax.axis_index("lon")
     span = ROWS * cols
     tile = 256
     hid = win.shape[1]
-    loads = [
-        pltpu.make_async_copy(win_hbm, win, load_sem.at[0]),
-        pltpu.make_async_copy(wout_hbm, wout, load_sem.at[1]),
-    ]
-    for i in range(chunks):
+    local = block.shape[2] // ROWS
+    total = chunks * ROWS
+    stride = band.shape[1]
+    freqs = forward.shape[1]
+    order = [0, chunks - 1] + list(range(1, chunks - 1))
+    loads = {"win": pltpu.make_async_copy(win_hbm, win, load_sem.at[0])}
+    loads["wout"] = pltpu.make_async_copy(wout_hbm, wout, load_sem.at[1])
+    for i in order:
         rows = pl.ds(i * span, span)
-        loads.append(pltpu.make_async_copy(tok_hbm.at[rows], tok.at[rows], load_sem.at[2 + 2 * i]))
-        loads.append(pltpu.make_async_copy(cot_hbm.at[rows], cot.at[rows], load_sem.at[3 + 2 * i]))
-    for load in loads:
+        loads["tok", i] = pltpu.make_async_copy(tok_hbm.at[rows], tok.at[rows], load_sem.at[2 + 2 * i])
+        loads["cot", i] = pltpu.make_async_copy(cot_hbm.at[rows], cot.at[rows], load_sem.at[3 + 2 * i])
+    for load in (loads["tok", 0], loads["win"], loads["cot", 0], loads["wout"]):
         load.start()
-    greet(lat, lon, peers, 0)
-    loads[0].wait()
-    loads[1].wait()
-
-    def send(i, peer):
-        return pltpu.make_async_remote_copy(
-            src_ref=packed.at[i, pl.ds(peer * cols, cols)],
-            dst_ref=moved.at[i, pl.ds(lon * cols, cols)],
-            send_sem=send_sem.at[i, peer],
-            recv_sem=recv_sem.at[i, lon],
+    for i in order[1:]:
+        loads["tok", i].start()
+        loads["cot", i].start()
+    loads["table"] = pltpu.make_async_copy(table_hbm, table, load_sem.at[2 + 2 * chunks])
+    loads["table"].start()
+    greet(lat, lon, peers, lat_count)
+
+    shift = lax.rem(near.shape[1] + reach - lat * total, near.shape[1])
+    columns = pltpu.roll(near[...], shift, 1)
+    live = pltpu.roll(widths[...], shift, 1)
+    target = lax.broadcasted_iota(jnp.int32, (total, near.shape[1]), 0) + lat * total
+    slots = weights.shape[1]
+    masks = [(columns[j : j + 1] == target) & (live > j) for j in range(slots)]
+    for k in range(basis_count):
+        lines = pltpu.roll(weights[k], shift, 1)
+        mixing = jnp.where(masks[0], lines[0:1], 0.0)
+        for j in range(1, slots):
+            mixing = mixing + jnp.where(masks[j], lines[j : j + 1], 0.0)
+        band[k * total : (k + 1) * total, :] = mixing[:, :stride].astype(jnp.bfloat16)
+    half_len = freqs // 2
+    cos_part, sin_part = spectrum[:, :half_len], spectrum[:, half_len:]
+    cos_rows = split_lanes(jnp.concatenate([cos_part, cos_part], 1), half_len)
+    sin_rows = split_lanes(jnp.concatenate([-sin_part, sin_part], 1), half_len)
+    for k in range(basis_count):
+        cosine[k] = jnp.broadcast_to(cos_rows[k : k + 1], (8, freqs))
+        sine[k] = jnp.broadcast_to(sin_rows[k : k + 1], (8, freqs))
+
+    def to_peer(i, peer):
+        return pltpu.make_async_remote_copy(
+            src_ref=moving.at[i, pl.ds(peer * cols, cols)],
+            dst_ref=block.at[i, pl.ds(lon * cols, cols)],
+            send_sem=to_sem.at[i, peer],
+            recv_sem=from_sem.at[i, lon],
             device_id=(lat, peer),
             device_id_type=MESH,
         )
 
-    def own(i):
+    def from_peer(i, peer):
+        return pltpu.make_async_remote_copy(
+            src_ref=moving.at[i, pl.ds(peer * cols, cols)],
+            dst_ref=block.at[i, pl.ds(peer * cols, cols)],
+            send_sem=to_sem.at[i, peer],
+            recv_sem=from_sem.at[i, peer],
+            device_id=(lat, peer),
+            device_id_type=MESH,
+        )
+
+    def keep(i):
         rows = pl.ds(lon * cols, cols)
-        return pltpu.make_async_copy(packed.at[i, rows], moved.at[i, rows], send_sem.at[i, lon])
-
-    for i in range(chunks):
+        return pltpu.make_async_copy(moving.at[i, rows], block.at[i, rows], to_sem.at[i, lon])
+
+    for i in order:
         rows = pl.ds(i * span, span)
-        loads[2 + 2 * i].wait()
-        loads[3 + 2 * i].wait()
+        loads["tok", i].wait()
+        if i == 0:
+            loads["win"].wait()
+        loads["cot", i].wait()
+        if i == 0:
+            loads["wout"].wait()
         here, cotan = tok[rows, :], cot[rows, :]
-
-        def column(j, carry):
-            at = pl.ds(pl.multiple_of(j * tile, tile), tile)
+        for j in range(hid // tile):
+            at = pl.ds(j * tile, tile)
             value = nn(here, win[:, at])
             back = nt(cotan, wout[at, :])
             square = value * value
@@ -267,30 +312,17 @@
             slope = gate * (1.0 + (1.0 - tangent) * (scaled * (1.0 + 0.134145 * square)))
             hidden[rows, at] = (value * gate).astype(jnp.bfloat16)
             grad[rows, at] = (back * slope).astype(jnp.bfloat16)
-            return carry
-
-        lax.fori_loop(0, hid // tile, column, 0)
         grid = (cotan.astype(jnp.float32) + nt(grad[rows, :], win[...])).astype(jnp.bfloat16)
-        blocks = [grid[r * cols : (r + 1) * cols] for r in range(ROWS)]
-        for at, block in enumerate(swap_blocks(blocks, grid.shape[1] // peers)):
-            packed[i, at * cols : (at + 1) * cols, :] = block
+        lines = [grid[r * cols : (r + 1) * cols] for r in range(ROWS)]
+        for at, line in enumerate(swap_blocks(lines, local)):
+            moving[i, at * cols : (at + 1) * cols, :] = line
         for step in range(1, peers):
-            send(i, lax.rem(lon + step, peers)).start()
-        own(i).start()
-
-    for i in range(chunks):
-        tok_t[:, i * span : (i + 1) * span] = tok[i * span : (i + 1) * span, :].T
-        cot_t[:, i * span : (i + 1) * span] = cot[i * span : (i + 1) * span, :].T
-
-    def products(j, carry):
-        at = pl.ds(pl.multiple_of(j * tile, tile), tile)
-        parts[0, at, :] = nn(tok_t[...], grad[:, at]).T.astype(jnp.bfloat16)
-        parts[1, at, :] = nn(cot_t[...], hidden[:, at]).T.astype(jnp.bfloat16)
-        return carry
-
-    lax.fori_loop(0, hid // tile, products, 0)
+            to_peer(i, lax.rem(lon + step, peers)).start()
+        keep(i).start()
+
     piece = hid // peers
-    core = lax.rem(lon, 2)
+    chips = peers // 2
+    chip, core = lax.div(lon, 2), lax.rem(lon, 2)
 
     def to_pair(kind, q):
         return pltpu.make_async_remote_copy(
@@ -302,52 +334,18 @@
             device_id_type=MESH,
         )
 
-    for q in range(peers // 2):
-        for kind in range(2):
+    for kind, source, target_t, other in ((0, tok, tok_t, grad), (1, cot, cot_t, hidden)):
+        for i in range(chunks):
+            target_t[:, i * span : (i + 1) * span] = source[i * span : (i + 1) * span, :].T
+
+        def products(j, carry):
+            at = pl.ds(pl.multiple_of(j * tile, tile), tile)
+            parts[kind, at, :] = nn(target_t[...], other[:, at]).T.astype(jnp.bfloat16)
+            return carry
+
+        lax.fori_loop(0, hid // tile, products, 0)
+        for q in range(chips):
             to_pair(kind, q).start()
-    for q in range(peers // 2):
-        for kind in range(2):
-            to_pair(kind, q).wait()
-            mine = parts[kind, pl.ds(pl.multiple_of((2 * q + core) * piece, 16), piece), :]
-            both = mine.astype(jnp.float32) + pair_in[q, kind].astype(jnp.float32)
-            half[q, kind] = both.astype(jnp.bfloat16)
-    for i in range(chunks):
-        own(i).wait()
-        for step in range(1, peers):
-            peer = lax.rem(lon + step, peers)
-            send(i, peer).wait_send()
-            pltpu.make_async_remote_copy(
-                src_ref=packed.at[i, pl.ds(peer * cols, cols)],
-                dst_ref=moved.at[i, pl.ds(peer * cols, cols)],
-                send_sem=send_sem.at[i, peer],
-                recv_sem=recv_sem.at[i, peer],
-                device_id=(lat, peer),
-                device_id_type=MESH,
-            ).wait_recv()
-
-
-def filter_kernel(
-    peers, cols, chunks, lat_count, reach, basis_count,
-    moved, cot_hbm, half, forward, inverse, band, cosine, sine, chan,
-    out, grad_in, grad_out,
-    block, cot, wide, turned, packed, landed, up_out, down_out, up_in, down_in,
-    lon_in, lat_out, lat_in,
-    load_sem, send_sem, recv_sem, halo_send, halo_recv,
-    lon_send, lon_recv, lat_send, lat_recv,
-):
-    lat, lon = lax.axis_index("lat"), lax.axis_index("lon")
-    local = block.shape[2] // ROWS
-    total = chunks * ROWS
-    stride = band.shape[1]
-    freqs = forward.shape[1]
-    loads = [pltpu.make_async_copy(moved.at[i], block.at[i], load_sem.at[i]) for i in range(chunks)]
-    cot_load = pltpu.make_async_copy(cot_hbm, cot, load_sem.at[chunks])
-    for load in loads:
-        load.start()
-    cot_load.start()
-    greet(lat, lon, peers, lat_count)
-    chips = peers // 2
-    chip, core = lax.div(lon, 2), lax.rem(lon, 2)
 
     def to_chip(other):
         return pltpu.make_async_remote_copy(
@@ -377,11 +375,14 @@
             device_id=(other, lon), device_id_type=MESH,
         )
 
+    loads["table"].wait()
+    lane = lax.broadcasted_iota(jnp.int32, (1, freqs), 1)
+    first = (lane == 0) | (lane == (LANES if half_len > LANES else half_len))
+    scaling = jnp.where(first, 1.0 / freqs, 2.0 / freqs)
+    forward[...] = table[...].astype(jnp.bfloat16)
+    inverse[...] = (table[...] * scaling).astype(jnp.bfloat16)
     chip_own = pltpu.make_async_copy(half.at[chip], lon_in.at[chip], lon_send.at[chip])
     lat_own = pltpu.make_async_copy(lat_out.at[lat], lat_in.at[lat], lat_send.at[lat])
-    chip_own.start()
-    for step in range(1, chips):
-        to_chip(lax.rem(chip + step, chips)).start()
     zero = jnp.zeros((local, freqs), jnp.float32)
     for r in range(total + 2 * reach, stride):
         for m in range(freqs // LANES):
@@ -402,9 +403,10 @@
 
     to_prev = halo(up_out, up_in, lat - 1, 0)
     to_next = halo(down_out, down_in, lat + 1, 1)
-    order = [0, chunks - 1] + list(range(1, chunks - 1))
     for i in order:
-        loads[i].wait()
+        keep(i).wait()
+        for step in range(1, peers):
+            from_peer(i, lax.rem(lon + step, peers)).wait_recv()
         spectra = tn(block[i], forward[...])
         place(spectra, reach + i * ROWS, ROWS)
         if i == 0:
@@ -420,6 +422,16 @@
             @pl.when(lat < lat_count - 1)
             def _():
                 to_next.start()
+
+    for q in range(chips):
+        for kind in range(2):
+            to_pair(kind, q).wait()
+            mine = parts[kind, pl.ds(pl.multiple_of((2 * q + core) * piece, 16), piece), :]
+            both = mine.astype(jnp.float32) + pair_in[q, kind].astype(jnp.float32)
+            half[q, kind] = both.astype(jnp.bfloat16)
+    for step in range(1, chips):
+        to_chip(lax.rem(chip + step, chips)).start()
+    chip_own.start()
 
     @pl.when(lat > 0)
     def _():
@@ -525,7 +537,6 @@
         sums.append(summed)
     grad_in[...] = sums[0]
     grad_out[...] = sums[1].T
-    cot_load.wait()
     for i in range(chunks):
         own(i).wait()
         for step in range(1, peers):
@@ -551,6 +562,7 @@
                 out[at, :] = (cot[at, :].astype(jnp.float32) + line.astype(jnp.float32)).astype(jnp.bfloat16)
     for i in range(chunks):
         for step in range(1, peers):
+            to_peer(i, lax.rem(lon + step, peers)).wait_send()
             send(i, lax.rem(lon + step, peers)).wait_send()
     for step in range(1, chips):
         to_chip(lax.rem(chip + step, chips)).wait_send()
@@ -585,19 +597,14 @@
     return jnp.concatenate(pieces, axis=1)
 
 
-def lon_tables(lon_total):
+def lon_table(lon_total):
     half_len = lon_total // 2
     order = split_order(half_len)
     frequency = order % half_len
     phases = (np.arange(lon_total)[:, None] * frequency[None, :]) % lon_total
     angles = phases * (2.0 * math.pi / lon_total)
     forward = np.where((order >= half_len)[None, :], np.sin(angles), np.cos(angles))
-    scaling = np.where(frequency == 0, 1.0, 2.0) / lon_total
-    inverse = forward * scaling[None, :]
-    return (
-        jnp.asarray(forward.astype(np.float32)).astype(jnp.bfloat16),
-        jnp.asarray(inverse.astype(np.float32)).astype(jnp.bfloat16),
-    )
+    return forward.astype(np.float32)
 
 
 def fast_body(
@@ -616,7 +623,6 @@
     span = ROWS * lon_cols
     tokens = lat_rows * lon_cols
     stride = -(-(lat_rows + 2 * reach) // 16) * 16
-    row_start = lax.axis_index("lat") * lat_rows
     any_spec = pl.BlockSpec(memory_space=pl.ANY)
     vmem_spec = pl.BlockSpec(memory_space=pltpu.VMEM)
     smem_spec = pl.BlockSpec(memory_space=pltpu.SMEM)
@@ -624,15 +630,26 @@
     tok_flat = mlp_input.reshape(tokens, channels)
     cot_flat = out_cot.reshape(tokens, channels)
 
-    with jax.named_scope("mlp"):
-        moved, half = pl.pallas_call(
-            functools.partial(mlp_kernel, peers, lon_cols, chunks),
+    table = jnp.asarray(lon_table(lon_total))
+    near = band_cols.T
+    weights = row_weights.transpose(0, 2, 1)
+    widths = band_widths.reshape(1, lat_total)
+    move_shape = (chunks, lon_total, ROWS * local)
+    piece, share = hid // peers, channels // lat_count
+    freqs = 2 * half_len
+    dma = pltpu.SemaphoreType.DMA
+    with jax.named_scope("exchange"):
+        out, grad_in, grad_out = pl.pallas_call(
+            functools.partial(
+                exchange_kernel, peers, lon_cols, chunks, lat_count, reach, basis_count
+            ),
             out_shape=(
-                jax.ShapeDtypeStruct((chunks, lon_total, ROWS * local), bf16),
-                jax.ShapeDtypeStruct((peers // 2, 2, hid // peers, channels), bf16),
+                jax.ShapeDtypeStruct((tokens, channels), bf16),
+                jax.ShapeDtypeStruct((share, piece), f32),
+                jax.ShapeDtypeStruct((piece, share), f32),
             ),
-            in_specs=[any_spec] * 4,
-            out_specs=(any_spec, vmem_spec),
+            in_specs=[any_spec] * 5 + [vmem_spec] * 4 + [smem_spec],
+            out_specs=(vmem_spec,) * 3,
             scratch_shapes=[
                 pltpu.VMEM((tokens, channels), bf16),
                 pltpu.VMEM((tokens, channels), bf16),
@@ -642,79 +659,37 @@
                 pltpu.VMEM((channels, tokens), bf16),
                 pltpu.VMEM((tokens, hid), bf16),
                 pltpu.VMEM((tokens, hid), bf16),
-                pltpu.VMEM((chunks, lon_total, ROWS * local), bf16),
+                pltpu.VMEM(move_shape, bf16),
+                pltpu.VMEM(move_shape, bf16),
                 pltpu.VMEM((2, hid, channels), bf16),
-                pltpu.VMEM((peers // 2, 2, hid // peers, channels), bf16),
-                pltpu.SemaphoreType.DMA((2 + 2 * chunks,)),
-                pltpu.SemaphoreType.DMA((chunks, peers)),
-                pltpu.SemaphoreType.DMA((chunks, peers)),
-                pltpu.SemaphoreType.DMA((peers // 2, 2)),
-                pltpu.SemaphoreType.DMA((peers // 2, 2)),
-            ],
+                pltpu.VMEM((peers // 2, 2, piece, channels), bf16),
+                pltpu.VMEM((peers // 2, 2, piece, channels), bf16),
+                pltpu.VMEM((basis_count * lat_rows, stride), bf16),
+                pltpu.VMEM((basis_count, 8, freqs), f32),
+                pltpu.VMEM((basis_count, 8, freqs), f32),
+                pltpu.VMEM((lon_total, freqs), f32),
+                pltpu.VMEM((lon_total, freqs), bf16),
+                pltpu.VMEM((lon_total, freqs), bf16),
+                pltpu.VMEM((freqs // LANES, local * stride, LANES), f32),
+                pltpu.VMEM((freqs // LANES, local * lat_rows, LANES), f32),
+                pltpu.VMEM(move_shape, bf16),
+                pltpu.VMEM(move_shape, bf16),
+            ]
+            + [pltpu.VMEM((reach * local, freqs), bf16)] * 4
+            + [pltpu.VMEM((peers // 2, 2, piece, channels), bf16)]
+            + [pltpu.VMEM((lat_count, 2, share, piece), bf16)] * 2
+            + [dma((3 + 2 * chunks,))]
+            + [dma((chunks, peers))] * 2
+            + [dma((peers // 2, 2))] * 2
+            + [dma((chunks, peers))] * 2
+            + [dma((2,))] * 2
+            + [dma((peers // 2,))] * 2
+            + [dma((lat_count,))] * 2,
             compiler_params=pltpu.CompilerParams(
-                collective_id=0, has_side_effects=True, vmem_limit_bytes=48 * 2**20
+                collective_id=0, has_side_effects=True, vmem_limit_bytes=VMEM_BYTES
             ),
-            name="mlp_exchange",
-        )(tok_flat, cot_flat, w_in, w_out)
-
-    with jax.named_scope("band"):
-        pad = ((reach, reach),)
-        near_cols = lax.dynamic_slice_in_dim(jnp.pad(band_cols, pad + ((0, 0),), constant_values=-1), row_start, lat_rows + 2 * reach, 0)
-        near_widths = lax.dynamic_slice_in_dim(jnp.pad(band_widths, pad), row_start, lat_rows + 2 * reach, 0)
-        near_weights = lax.dynamic_slice_in_dim(
-            jnp.pad(row_weights, ((0, 0),) + pad + ((0, 0),)), row_start, lat_rows + 2 * reach, 1
-        )
-        targets = row_start + jnp.arange(lat_rows, dtype=jnp.int32)
-        band = jnp.zeros((basis_count, lat_rows, lat_rows + 2 * reach), f32)
-        for j in range(slots):
-            live = (near_cols[None, :, j] == targets[:, None]) & (j < near_widths)[None, :]
-            band = band + jnp.where(live[None], near_weights[:, None, :, j], 0.0)
-        band = jnp.pad(band, ((0, 0), (0, 0), (0, stride - lat_rows - 2 * reach)))
-        band = band.reshape(basis_count * lat_rows, stride).astype(bf16)
-        cos_part, sin_part = basis_spectra[:, :half_len], basis_spectra[:, half_len:]
-        cosine = split_lanes(jnp.concatenate([cos_part, cos_part], 1), half_len)
-        sine = split_lanes(jnp.concatenate([-sin_part, sin_part], 1), half_len)
-        cosine = jnp.broadcast_to(cosine[:, None, :], (basis_count, 8, 2 * half_len))
-        sine = jnp.broadcast_to(sine[:, None, :], (basis_count, 8, 2 * half_len))
-        forward, inverse = lon_tables(lon_total)
-
-    with jax.named_scope("filter"):
-        out, grad_in, grad_out = pl.pallas_call(
-            functools.partial(filter_kernel, peers, lon_cols, chunks, lat_count, reach, basis_count),
-            out_shape=(
-                jax.ShapeDtypeStruct((tokens, channels), bf16),
-                jax.ShapeDtypeStruct((channels // lat_count, hid // peers), f32),
-                jax.ShapeDtypeStruct((hid // peers, channels // lat_count), f32),
-            ),
-            in_specs=[any_spec] * 3 + [vmem_spec] * 5 + [smem_spec],
-            out_specs=(vmem_spec,) * 3,
-            scratch_shapes=[
-                pltpu.VMEM((chunks, lon_total, ROWS * local), bf16),
-                pltpu.VMEM((tokens, channels), bf16),
-                pltpu.VMEM((2 * half_len // LANES, local * stride, LANES), f32),
-                pltpu.VMEM((2 * half_len // LANES, local * lat_rows, LANES), f32),
-                pltpu.VMEM((chunks, lon_total, ROWS * local), bf16),
-                pltpu.VMEM((chunks, lon_total, ROWS * local), bf16),
-            ]
-            + [pltpu.VMEM((reach * local, 2 * half_len), bf16)] * 4
-            + [pltpu.VMEM((peers // 2, 2, hid // peers, channels), bf16)]
-            + [pltpu.VMEM((lat_count, 2, channels // lat_count, hid // peers), bf16)] * 2
-            + [
-                pltpu.SemaphoreType.DMA((chunks + 1,)),
-                pltpu.SemaphoreType.DMA((chunks, peers)),
-                pltpu.SemaphoreType.DMA((chunks, peers)),
-                pltpu.SemaphoreType.DMA((2,)),
-                pltpu.SemaphoreType.DMA((2,)),
-                pltpu.SemaphoreType.DMA((peers // 2,)),
-                pltpu.SemaphoreType.DMA((peers // 2,)),
-                pltpu.SemaphoreType.DMA((lat_count,)),
-                pltpu.SemaphoreType.DMA((lat_count,)),
-            ],
-            compiler_params=pltpu.CompilerParams(
-                collective_id=1, has_side_effects=True, vmem_limit_bytes=48 * 2**20
-            ),
-            name="filter_exchange",
-        )(moved, cot_flat, half, forward, inverse, band, cosine, sine, chan_weights)
+            name="exchange",
+        )(tok_flat, cot_flat, w_in, w_out, table, weights, near, widths, basis_spectra, chan_weights)
     return (out.reshape(lat_rows, lon_cols, channels), grad_in, grad_out)
 
 
@@ -728,6 +703,7 @@
         peers > 2
         and peers % 2 == 0
         and lat_count > 1
+        and lat_total == LANES
         and (lat_rows // ROWS) % GROUPS == 0
         and local % (4 * GROUPS) == 0
         and (hid // peers) % 16 == 0

time: 91.3 us -> 83.5 us (0.915)
  local copies, waits for them, and re-layouts: 9.2 us -> 4.37 us
  other arithmetic: 1.91 us -> 0 us
    unnamed x14 -> x7, local copies, waits for them, and re-layouts: 6.37 us -> 4.37 us
    slice x4 -> x0, local copies, waits for them, and re-layouts: 1.59 us -> none  [the longest x1 0.79 us: split_lanes(): values[:, half_len + m * LANES:half_len + (m + 1) * LANES]]
    eq x1 -> x0, local copies, waits for them, and re-layouts: 1.09 us -> none  [fast_body(): near_cols[None, :, j] == targets[:, None]]
    pallas_call x2 -> x1, Pallas kernels: 79 us -> 78.3 us  [fast_body(): pl.pallas_call(functools.partial(exchange_kernel, peers, lon_cols, chunks...]
where the time goes in v2:
time: 83.5 us; the launch traced here: 83.3 us
  Pallas kernels  78.3 us (94%)
  local copies, waits for them, and re-layouts  4.37 us (5%)
    pallas_call x1, Pallas kernels, fast_body(): pl.pallas_call(functools.partial(exchange_kernel, peers, lon_cols, chunks...  78.3 us
    unnamed x7, local copies, waits for them, and re-layouts  4.37 us

profile of v2, /device:TPU:1, one launch (start us, length us, event | category | flops | bytes accessed | tf_op | source)
XLA Modules:
  0.0 83.3 jit_solution(9439878932231045934)
XLA Ops:
  0.6 78.3 %exchange.1 = (bf16[1536,640]{1,0:T(8,128)(2,1)}, f32[160,160]{1,0:T(8,128)}, f32[160,160]{1,0:T(8,128)}) custom-call(bf16[1536,640]{1,0:T(8,128)(2,1)} %bitcast.7, bf16[1536,640]{1,0:T(8,128)(2,1)} %bitcast.8, bf16[640,1280]{1,0:T(8,128)(2,1)} %win_hbm.1, bf16[1280,640]{1,0:T(8,128)(2,1)} %wout_hbm.1, f32[384,384]{1,0:T(8,128)} %constant.2.clone.table_hbm, ...), custom_call_target="tpu_custom_call" | custom-call | tf_op jit(solution)/shard_map/exchange/exchange/pallas_call | solution.py:642
  78.9 0.0 copy-start.1
  78.9 0.0 copy-start
  78.9 3.0 %copy.16 = bf16[32,48,640]{2,1,0:T(8,128)(2,1)} copy(bf16[32,48,640]{2,1,0:T(8,128)(2,1)} %bitcast.6) | data formatting | bytes 3932160
  82.0 0.0 copy-done.1
  82.0 0.7 copy.17
  82.6 0.0 copy-done
  82.6 0.7 copy.18
Async XLA Ops:
  78.9 3.1 %copy-start.1 = (f32[160,160]{1,0:T(8,128)S(1)}, f32[160,160]{1,0:T(8,128)}, u32[]{:S(2)}) copy-start(f32[160,160]{1,0:T(8,128)} %get-tuple-element.13) | copy-start | bytes 307204
  78.9 3.7 %copy-start = (f32[160,160]{1,0:T(8,128)S(1)}, f32[160,160]{1,0:T(8,128)}, u32[]{:S(2)}) copy-start(f32[160,160]{1,0:T(8,128)} %get-tuple-element.14) | copy-start | bytes 307204

commit v3 on v2

--- a/solution.py
+++ b/solution.py
@@ -172,8 +172,9 @@
 
 MESH = pl.DeviceIdType.MESH
 ROWS = 8
-GROUPS = 2
-VMEM_BYTES = 62 * 2**20
+GROUPS = 4
+TOGETHER = 10
+VMEM_BYTES = 56 * 2**20
 LANES = 128
 SLOPE = 0.7978845608
 
@@ -404,6 +405,17 @@
     to_prev = halo(up_out, up_in, lat - 1, 0)
     to_next = halo(down_out, down_in, lat + 1, 1)
     for i in order:
+        if i == order[2]:
+            for q in range(chips):
+                for kind in range(2):
+                    to_pair(kind, q).wait()
+                    mine = parts[kind, pl.ds(pl.multiple_of((2 * q + core) * piece, 16), piece), :]
+                    both = mine.astype(jnp.float32) + pair_in[q, kind].astype(jnp.float32)
+                    half[q, kind] = both.astype(jnp.bfloat16)
+            for step in range(1, chips):
+                to_chip(lax.rem(chip + step, chips)).start()
+            chip_own.start()
+
         keep(i).wait()
         for step in range(1, peers):
             from_peer(i, lax.rem(lon + step, peers)).wait_recv()
@@ -423,16 +435,6 @@
             def _():
                 to_next.start()
 
-    for q in range(chips):
-        for kind in range(2):
-            to_pair(kind, q).wait()
-            mine = parts[kind, pl.ds(pl.multiple_of((2 * q + core) * piece, 16), piece), :]
-            both = mine.astype(jnp.float32) + pair_in[q, kind].astype(jnp.float32)
-            half[q, kind] = both.astype(jnp.bfloat16)
-    for step in range(1, chips):
-        to_chip(lax.rem(chip + step, chips)).start()
-    chip_own.start()
-
     @pl.when(lat > 0)
     def _():
         to_next.wait_recv()
@@ -453,7 +455,7 @@
 
     first_chan = lon * local
     part = local // GROUPS
-    together = 4
+    together = TOGETHER
 
     def send(i, peer):
         return pltpu.make_async_remote_copy(
@@ -623,7 +625,7 @@
     span = ROWS * lon_cols
     tokens = lat_rows * lon_cols
     stride = -(-(lat_rows + 2 * reach) // 16) * 16
-    any_spec = pl.BlockSpec(memory_space=pl.ANY)
+    hbm_spec = pl.BlockSpec(memory_space=pltpu.HBM)
     vmem_spec = pl.BlockSpec(memory_space=pltpu.VMEM)
     smem_spec = pl.BlockSpec(memory_space=pltpu.SMEM)
     bf16, f32 = jnp.bfloat16, jnp.float32
@@ -648,7 +650,7 @@
                 jax.ShapeDtypeStruct((share, piece), f32),
                 jax.ShapeDtypeStruct((piece, share), f32),
             ),
-            in_specs=[any_spec] * 5 + [vmem_spec] * 4 + [smem_spec],
+            in_specs=[hbm_spec] * 5 + [vmem_spec] * 4 + [smem_spec],
             out_specs=(vmem_spec,) * 3,
             scratch_shapes=[
                 pltpu.VMEM((tokens, channels), bf16),
@@ -704,8 +706,9 @@
         and peers % 2 == 0
         and lat_count > 1
         and lat_total == LANES
+        and lat_rows >= 4 * ROWS
         and (lat_rows // ROWS) % GROUPS == 0
-        and local % (4 * GROUPS) == 0
+        and local % (TOGETHER * GROUPS) == 0
         and (hid // peers) % 16 == 0
         and channels % (16 * lat_count) == 0
         and lat_rows % 8 == 0

time: 83.5 us -> 82.5 us (0.988)
  Pallas kernels: 78.3 us -> 77.3 us
    pallas_call x1, Pallas kernels: 78.3 us -> 77.3 us  [fast_body(): pl.pallas_call(functools.partial(exchange_kernel, peers, lon_cols, chunks...]
where the time goes in v3:
time: 82.5 us; the launch traced here: 82.3 us
  Pallas kernels  77.3 us (94%)
  local copies, waits for them, and re-layouts  4.37 us (5%)
    pallas_call x1, Pallas kernels, fast_body(): pl.pallas_call(functools.partial(exchange_kernel, peers, lon_cols, chunks...  77.3 us
    unnamed x7, local copies, waits for them, and re-layouts  4.37 us

profile of v3, /device:TPU:1, one launch (start us, length us, event | category | flops | bytes accessed | tf_op | source)
XLA Modules:
  0.0 82.3 jit_solution(15738502680426363430)
XLA Ops:
  0.6 77.3 %exchange.1 = (bf16[1536,640]{1,0:T(8,128)(2,1)}, f32[160,160]{1,0:T(8,128)}, f32[160,160]{1,0:T(8,128)}) custom-call(bf16[1536,640]{1,0:T(8,128)(2,1)} %bitcast.7, bf16[1536,640]{1,0:T(8,128)(2,1)} %bitcast.8, bf16[640,1280]{1,0:T(8,128)(2,1)} %win_hbm.1, bf16[1280,640]{1,0:T(8,128)(2,1)} %wout_hbm.1, f32[384,384]{1,0:T(8,128)} %constant.2.clone.table_hbm, ...), custom_call_target="tpu_custom_call" | custom-call | tf_op jit(solution)/shard_map/exchange/exchange/pallas_call | solution.py:644
  77.9 0.0 copy-start.1
  77.9 0.0 copy-start
  77.9 3.0 %copy.16 = bf16[32,48,640]{2,1,0:T(8,128)(2,1)} copy(bf16[32,48,640]{2,1,0:T(8,128)(2,1)} %bitcast.6) | data formatting | bytes 3932160
  81.0 0.0 copy-done.1
  81.0 0.7 copy.17
  81.6 0.0 copy-done
  81.6 0.7 copy.18
Async XLA Ops:
  77.9 3.1 %copy-start.1 = (f32[160,160]{1,0:T(8,128)S(1)}, f32[160,160]{1,0:T(8,128)}, u32[]{:S(2)}) copy-start(f32[160,160]{1,0:T(8,128)} %get-tuple-element.13) | copy-start | bytes 307204
  77.9 3.7 %copy-start = (f32[160,160]{1,0:T(8,128)S(1)}, f32[160,160]{1,0:T(8,128)}, u32[]{:S(2)}) copy-start(f32[160,160]{1,0:T(8,128)} %get-tuple-element.14) | copy-start | bytes 307204

commit v4 on v3

--- a/solution.py
+++ b/solution.py
@@ -173,7 +173,7 @@
 MESH = pl.DeviceIdType.MESH
 ROWS = 8
 GROUPS = 4
-TOGETHER = 10
+TOGETHER = 5
 VMEM_BYTES = 56 * 2**20
 LANES = 128
 SLOPE = 0.7978845608
@@ -218,7 +218,7 @@
     tok_hbm, cot_hbm, win_hbm, wout_hbm, table_hbm, weights, near, widths, spectrum, chan,
     out, grad_in, grad_out,
     tok, cot, win, wout, tok_t, cot_t, hidden, grad, moving, block, parts, pair_in, half,
-    band, cosine, sine, table, forward, inverse,
+    band, cosine, sine, chan_t, gains, table, forward, inverse,
     wide, turned, packed, landed, up_out, down_out, up_in, down_in,
     lon_in, lat_out, lat_in,
     load_sem, to_sem, from_sem, pair_send, pair_recv,
@@ -231,7 +231,7 @@
     hid = win.shape[1]
     local = block.shape[2] // ROWS
     total = chunks * ROWS
-    stride = band.shape[1]
+    stride = band.shape[1] // basis_count
     freqs = forward.shape[1]
     order = [0, chunks - 1] + list(range(1, chunks - 1))
     loads = {"win": pltpu.make_async_copy(win_hbm, win, load_sem.at[0])}
@@ -255,19 +255,26 @@
     target = lax.broadcasted_iota(jnp.int32, (total, near.shape[1]), 0) + lat * total
     slots = weights.shape[1]
     masks = [(columns[j : j + 1] == target) & (live > j) for j in range(slots)]
+    pieces = []
     for k in range(basis_count):
         lines = pltpu.roll(weights[k], shift, 1)
         mixing = jnp.where(masks[0], lines[0:1], 0.0)
         for j in range(1, slots):
             mixing = mixing + jnp.where(masks[j], lines[j : j + 1], 0.0)
-        band[k * total : (k + 1) * total, :] = mixing[:, :stride].astype(jnp.bfloat16)
+        pieces.append(mixing[:, :stride])
+    band[...] = jnp.concatenate(pieces, axis=1)
+    chan_t[...] = chan[...].T
+    own_chan = chan_t[pl.ds(pl.multiple_of(lon * local, 8), local), :]
+    gains[...] = jnp.concatenate(
+        [jnp.broadcast_to(own_chan[:, k : k + 1], (local, stride)) for k in range(basis_count)], axis=1
+    )
     half_len = freqs // 2
     cos_part, sin_part = spectrum[:, :half_len], spectrum[:, half_len:]
     cos_rows = split_lanes(jnp.concatenate([cos_part, cos_part], 1), half_len)
-    sin_rows = split_lanes(jnp.concatenate([-sin_part, sin_part], 1), half_len)
+    sin_rows = split_lanes(jnp.concatenate([sin_part, -sin_part], 1), half_len)
     for k in range(basis_count):
-        cosine[k] = jnp.broadcast_to(cos_rows[k : k + 1], (8, freqs))
-        sine[k] = jnp.broadcast_to(sin_rows[k : k + 1], (8, freqs))
+        cosine[k] = jnp.broadcast_to(cos_rows[k : k + 1], (16, freqs)).astype(jnp.bfloat16)
+        sine[k] = jnp.broadcast_to(sin_rows[k : k + 1], (16, freqs)).astype(jnp.bfloat16)
 
     def to_peer(i, peer):
         return pltpu.make_async_remote_copy(
@@ -453,7 +460,6 @@
     def _():
         place(jnp.zeros((reach * local, freqs), jnp.float32), reach + total, reach)
 
-    first_chan = lon * local
     part = local // GROUPS
     together = TOGETHER
 
@@ -479,27 +485,26 @@
                 inner = step * together + u
                 c = group * part + inner
                 rows = pl.ds(pl.multiple_of(c * stride, stride), stride)
-                lines = jnp.concatenate(
-                    [wide[m, rows, :].astype(jnp.bfloat16) for m in range(tiles)], axis=1
+                straight = [wide[m, rows, :] for m in range(tiles)]
+                crossed = [straight[m + 1 - 2 * (m % 2)] for m in range(tiles - 1)]
+                crossed.append(pltpu.roll(straight[-1], LANES // 2, 1))
+                straight = jnp.concatenate([line.astype(jnp.bfloat16) for line in straight], axis=1)
+                crossed = jnp.concatenate([line.astype(jnp.bfloat16) for line in crossed], axis=1)
+                straight = straight.reshape(stride // 16, 16, freqs)
+                crossed = crossed.reshape(stride // 16, 16, freqs)
+                mixed = jnp.concatenate(
+                    [
+                        (cosine[k][None] * straight + sine[k][None] * crossed).reshape(stride, freqs)
+                        for k in range(basis_count)
+                    ],
+                    axis=0,
                 )
-                terms = nn(band[...], lines).reshape(basis_count, total // 8, 8, freqs)
-                straight = crossed = None
-                for k in range(basis_count):
-                    gain = chan[k, first_chan + c]
-                    one = (gain * cosine[k])[None] * terms[k]
-                    two = (gain * sine[k])[None] * terms[k]
-                    straight = one if k == 0 else straight + one
-                    crossed = two if k == 0 else crossed + two
-                straight = straight.reshape(total, freqs)
-                crossed = crossed.reshape(total, freqs)
+                mixing = (band[...] * gains[pl.ds(c, 1), :]).astype(jnp.bfloat16)
+                rows_out = nn(mixing, mixed)
                 for m in range(tiles):
-                    here = straight[:, m * LANES : (m + 1) * LANES]
-                    if m == tiles - 1:
-                        other = pltpu.roll(crossed[:, m * LANES :], LANES // 2, 1)
-                    else:
-                        pair = m + 1 - 2 * (m % 2)
-                        other = crossed[:, pair * LANES : (pair + 1) * LANES]
-                    turned[m, pl.ds(group * part * total + inner, total, stride=part), :] = here + other
+                    turned[m, pl.ds(group * part * total + inner, total, stride=part), :] = rows_out[
+                        :, m * LANES : (m + 1) * LANES
+                    ]
             return carry
 
         lax.fori_loop(0, part // together, channels, 0)
@@ -627,7 +632,6 @@
     stride = -(-(lat_rows + 2 * reach) // 16) * 16
     hbm_spec = pl.BlockSpec(memory_space=pltpu.HBM)
     vmem_spec = pl.BlockSpec(memory_space=pltpu.VMEM)
-    smem_spec = pl.BlockSpec(memory_space=pltpu.SMEM)
     bf16, f32 = jnp.bfloat16, jnp.float32
     tok_flat = mlp_input.reshape(tokens, channels)
     cot_flat = out_cot.reshape(tokens, channels)
@@ -650,7 +654,7 @@
                 jax.ShapeDtypeStruct((share, piece), f32),
                 jax.ShapeDtypeStruct((piece, share), f32),
             ),
-            in_specs=[hbm_spec] * 5 + [vmem_spec] * 4 + [smem_spec],
+            in_specs=[hbm_spec] * 5 + [vmem_spec] * 5,
             out_specs=(vmem_spec,) * 3,
             scratch_shapes=[
                 pltpu.VMEM((tokens, channels), bf16),
@@ -666,9 +670,11 @@
                 pltpu.VMEM((2, hid, channels), bf16),
                 pltpu.VMEM((peers // 2, 2, piece, channels), bf16),
                 pltpu.VMEM((peers // 2, 2, piece, channels), bf16),
-                pltpu.VMEM((basis_count * lat_rows, stride), bf16),
-                pltpu.VMEM((basis_count, 8, freqs), f32),
-                pltpu.VMEM((basis_count, 8, freqs), f32),
+                pltpu.VMEM((lat_rows, basis_count * stride), f32),
+                pltpu.VMEM((basis_count, 16, freqs), bf16),
+                pltpu.VMEM((basis_count, 16, freqs), bf16),
+                pltpu.VMEM((channels, basis_count), f32),
+                pltpu.VMEM((local, basis_count * stride), f32),
                 pltpu.VMEM((lon_total, freqs), f32),
                 pltpu.VMEM((lon_total, freqs), bf16),
                 pltpu.VMEM((lon_total, freqs), bf16),

time: 82.5 us -> 82.2 us (level)
  no operation moved by 1% of the time
where the time goes in v4:
time: 82.2 us; the launch traced here: 82 us
  Pallas kernels  77 us (94%)
  local copies, waits for them, and re-layouts  4.37 us (5%)
    pallas_call x1, Pallas kernels, fast_body(): pl.pallas_call(functools.partial(exchange_kernel, peers, lon_cols, chunks...  77 us
    unnamed x7, local copies, waits for them, and re-layouts  4.37 us

profile of v4, /device:TPU:1, one launch (start us, length us, event | category | flops | bytes accessed | tf_op | source)
XLA Modules:
  0.0 82.0 jit_solution(15013876845014602783)
XLA Ops:
  0.6 77.0 %exchange.1 = (bf16[1536,640]{1,0:T(8,128)(2,1)}, f32[160,160]{1,0:T(8,128)}, f32[160,160]{1,0:T(8,128)}) custom-call(bf16[1536,640]{1,0:T(8,128)(2,1)} %bitcast.7, bf16[1536,640]{1,0:T(8,128)(2,1)} %bitcast.8, bf16[640,1280]{1,0:T(8,128)(2,1)} %win_hbm.1, bf16[1280,640]{1,0:T(8,128)(2,1)} %wout_hbm.1, f32[384,384]{1,0:T(8,128)} %constant.2.clone.table_hbm, ...), custom_call_target="tpu_custom_call" | custom-call | tf_op jit(solution)/shard_map/exchange/exchange/pallas_call | solution.py:648
  77.7 0.0 copy-start.1
  77.7 0.0 copy-start
  77.7 3.0 %copy.16 = bf16[32,48,640]{2,1,0:T(8,128)(2,1)} copy(bf16[32,48,640]{2,1,0:T(8,128)(2,1)} %bitcast.6) | data formatting | bytes 3932160
  80.7 0.0 copy-done.1
  80.7 0.7 copy.17
  81.4 0.0 copy-done
  81.4 0.7 copy.18
Async XLA Ops:
  77.7 3.1 %copy-start.1 = (f32[160,160]{1,0:T(8,128)S(1)}, f32[160,160]{1,0:T(8,128)}, u32[]{:S(2)}) copy-start(f32[160,160]{1,0:T(8,128)} %get-tuple-element.13) | copy-start | bytes 307204
  77.7 3.7 %copy-start = (f32[160,160]{1,0:T(8,128)S(1)}, f32[160,160]{1,0:T(8,128)}, u32[]{:S(2)}) copy-start(f32[160,160]{1,0:T(8,128)} %get-tuple-element.14) | copy-start | bytes 307204
